TPU v7x, 512 devices: a whole 4x4x16 slice. The times are simulated.
512 devices in a mesh: chan: 32 (over y, z_hi, core), freq: 16 (over z_lo, x).
Axes of the slice: x: 4, y: 4, z: 16 (z_hi: 4, z_lo: 4; z = z_hi * 4 + z_lo), core: 2. Of those that a mesh axis runs over, the one named last changes fastest.
Arguments:
- traces: bfloat16 [139264, 4096], P('freq', 'chan'), may hold values from -6 to 6
- kept_bins: int32 [128], replicated, may hold values from 1 to 511, as said below
- window_starts: int32 [256], P('freq'), may hold values from 0 to 7680, as said below
Outputs:
- stacked: bfloat16 [4, 2, 128, 4096, 128], P(None, None, 'freq', 'chan')
Inputs may be any that keep to these rules, and one draw needn't show every extreme that they name: `kept_bins`: the 128 numbers are distinct; 1 and 511 are always among them. `window_starts`: in each time block of 16 windows the first window starts at 0 and the last at 7680.
All inputs are finite; a program needn't handle non-finite values.
Results may differ from a plain program's by a relative error of at most 0.0064.
Values may be sent and summed in bfloat16 or wider, within the bound.
No kernel may reach another device: no remote copies, remote signals or barrier semaphores. Data moves between devices by JAX's collectives and lax.ppermute only.
A program may use at most 64 MiB of HBM per device.

v0:
```python
import math

import jax
import jax.numpy as jnp
from jax import lax
from jax.sharding import PartitionSpec as P

L = 1024
ROUNDS = 4


def partner(block, axis, distance):
    count = lax.axis_size(axis)
    route = []
    for low in range(count):
        high = low | 1 << distance
        if high != low and high < count:
            route += [(low, high), (high, low)]
    return lax.ppermute(block, axis, route)


def dft_rows(kept_bins, length):
    sample = jnp.arange(length, dtype=jnp.int32)
    phase = kept_bins[:, None] * sample[None, :] % length
    angle = phase.astype(jnp.float32) * (2.0 * math.pi / length)
    rows = jnp.stack([jnp.cos(angle), -jnp.sin(angle)], axis=1)
    return rows.reshape(2 * kept_bins.shape[0], length).astype(jnp.bfloat16)


def hann_taper(length):
    sample = jnp.arange(length, dtype=jnp.float32)
    return 0.5 - 0.5 * jnp.cos(sample * (2.0 * math.pi / length))


def spectra_local(windows, dft_table):
    values = windows.astype(jnp.float32)
    values = values - jnp.mean(values, axis=1, keepdims=True)
    tapered = (values * hann_taper(windows.shape[1])[None, :, None]).astype(jnp.bfloat16)
    spectra = jnp.einsum("jn,wnc->jwc", dft_table, tapered, preferred_element_type=jnp.float32)
    spectra = spectra.reshape(dft_table.shape[0] // 2, 2, windows.shape[0], windows.shape[2])
    power = jnp.mean(spectra * spectra, axis=(0, 1))
    return (spectra * lax.rsqrt(power + 1e-06)).astype(jnp.bfloat16)


def cross_spectra(own_spec, far_spec):
    prods = jnp.einsum("kcwa,kdwb->cdkab", own_spec, far_spec, preferred_element_type=jnp.float32)
    real_part = prods[0, 0] + prods[1, 1]
    imag_part = prods[1, 0] - prods[0, 1]
    scale = 1.0 / math.sqrt(own_spec.shape[2])
    return (jnp.stack([real_part, imag_part]) * scale).astype(jnp.bfloat16)


def send_whole(block_spec, mask_value):
    for bit_number in range(mask_value.bit_length()):
        if mask_value >> bit_number & 1:
            block_spec = partner(block_spec, "chan", bit_number)
    return block_spec


def per_device(traces, kept_bins, window_starts):
    dft_table = dft_rows(kept_bins, L)
    sample_index = window_starts[:, None] + jnp.arange(L, dtype=jnp.int32)[None, :]
    windows = traces[sample_index]
    white = spectra_local(windows, dft_table)
    turned = lax.all_to_all(white, "freq", split_axis=0, concat_axis=2, tiled=True)
    outputs = []
    for round_number in range(ROUNDS):
        mask_value = round_number + 1
        far_spec = send_whole(turned, mask_value)
        outputs.append(cross_spectra(turned, far_spec))
    return jnp.stack(outputs)


def solution(mesh):
    return jax.shard_map(
        per_device,
        mesh=mesh,
        in_specs=(P("freq", "chan"), P(), P("freq")),
        out_specs=P(None, None, "freq", "chan", None),
        check_vma=False,
    )
```

profile of v0, /device:TPU:6, one launch (start us, length us, event | category | flops | bytes accessed | tf_op | source)
XLA Modules:
  0.0 388.7 jit_solution(7465625569074371974)
XLA Ops:
  0.0 0.0 copy-start
  0.1 0.9 fusion.23
  1.0 0.7 copy-done
  1.6 57.4 %gather_fusion = bf16[16384,128]{1,0:T(8,128)(2,1)} fusion(bf16[8704,128]{1,0:T(8,128)(2,1)S(1)} %copy-done, s32[16384]{0:T(1024)S(1)} %broadcast_clamp_fusion), kind=kCustom, calls=%fused_computation | custom fusion | bytes 8454144 | tf_op jit(solution)/shard_map/gather | solution.py:63
  59.1 2.9 convert_reduce_fusion
  62.0 0.0 copy-done.2
  62.0 2.4 cosine_convert_fusion
  64.4 1.5 multiply_reduce_fusion
  65.9 0.2 multiply_convert_fusion
  66.2 0.7 copy.16
  66.9 33.4 %all_to_all.18 = bf16[128,2,16,128]{3,2,1,0:T(8,128)(2,1)S(1)} all-to-all(bf16[128,2,16,128]{3,2,1,0:T(8,128)(2,1)S(1)} %copy.16), channel_id=1, replica_groups=mesh['chan'=32,'freq'=16] {'freq'}, dimensions={0} | all-to-all | bytes 2097152 | tf_op jit(solution)/shard_map/all_to_all | solution.py:65
  100.3 0.3 copy.17
  100.5 1.9 collective-permute-start
  102.5 9.1 %collective-permute-start.1 = (bf16[8,2,256,128]{3,2,1,0:T(8,128)(2,1)S(1)}, bf16[8,2,256,128]{3,2,1,0:T(8,128)(2,1)S(1)}, u32[]{:S(2)}, u32[]{:S(2)}) collective-permute-start(bf16[8,2,256,128]{3,2,1,0:T(8,128)(2,1)S(1)} %bitcast.60), channel_id=1, source_target_pairs={{0,32},{32,0},{16,48},{48,16},{64,96},{96,64},{80,112},{112,80},{1... | collective-permute-start | bytes 3145736 | tf_op jit(solution)/shard_map/ppermute | solution.py:19
  111.6 8.2 %collective-permute-start.3 = (bf16[8,2,256,128]{3,2,1,0:T(8,128)(2,1)S(1)}, bf16[8,2,256,128]{3,2,1,0:T(8,128)(2,1)S(1)}, u32[]{:S(2)}, u32[]{:S(2)}) collective-permute-start(bf16[8,2,256,128]{3,2,1,0:T(8,128)(2,1)S(1)} %bitcast.61), channel_id=1, source_target_pairs={{0,64},{64,0},{16,80},{80,16},{32,96},{96,32},{48,112},{112,48},{1... | collective-permute-start | bytes 3145736 | tf_op jit(solution)/shard_map/ppermute | solution.py:19
  119.8 0.0 collective-permute-done
  119.8 5.5 %collective-permute-start.2 = (bf16[8,2,256,128]{3,2,1,0:T(8,128)(2,1)S(1)}, bf16[8,2,256,128]{3,2,1,0:T(8,128)(2,1)S(1)}, u32[]{:S(2)}, u32[]{:S(2)}) collective-permute-start(bf16[8,2,256,128]{3,2,1,0:T(8,128)(2,1)S(1)} %collective-permute-done), channel_id=1, source_target_pairs={{0,32},{32,0},{16,48},{48,16},{64,96},{96,64},{80,112},{112,80},{1... | collective-permute-start | bytes 3145736 | tf_op jit(solution)/shard_map/ppermute | solution.py:19
  125.3 0.5 convolution_bitcast_fusion.3
  125.8 234.0 %collective-permute-done.1 = bf16[8,2,256,128]{3,2,1,0:T(8,128)(2,1)S(1)} collective-permute-done((bf16[8,2,256,128]{3,2,1,0:T(8,128)(2,1)S(1)}, bf16[8,2,256,128]{3,2,1,0:T(8,128)(2,1)S(1)}, u32[]{:S(2)}, u32[]{:S(2)}) %collective-permute-start.1) | collective-permute-done | bytes 1048608 | tf_op jit(solution)/shard_map/ppermute | solution.py:19
  359.8 0.5 convolution_bitcast_fusion.2
  360.3 0.1 slice_add_fusion.3
  360.4 0.1 slice_add_fusion.2
  360.6 0.3 fusion.7
  360.8 0.0 collective-permute-done.3
  360.8 0.5 convolution_bitcast_fusion
  361.3 0.1 slice_add_fusion
  361.5 20.8 %collective-permute-done.2 = bf16[8,2,256,128]{3,2,1,0:T(8,128)(2,1)S(1)} collective-permute-done((bf16[8,2,256,128]{3,2,1,0:T(8,128)(2,1)S(1)}, bf16[8,2,256,128]{3,2,1,0:T(8,128)(2,1)S(1)}, u32[]{:S(2)}, u32[]{:S(2)}) %collective-permute-start.2) | collective-permute-done | bytes 1048608 | tf_op jit(solution)/shard_map/ppermute | solution.py:19
  382.3 0.5 convolution_bitcast_fusion.1
  382.8 0.1 slice_add_fusion.1
  382.9 0.3 fusion.9
  383.2 1.6 pad_maximum_fusion
  384.8 3.9 %copy.22 = bf16[4,2,8,128,128]{4,3,2,1,0:T(8,128)(2,1)} copy(bf16[4,2,8,128,128]{3,4,0,1,2:T(8,128)(2,1)} %pad_maximum_fusion) | data formatting | bytes 4194304 | tf_op jit(solution)/shard_map/stack | solution.py:71
  (8 shorter events, 0.1 us)
Async XLA Ops:
  0.0 1.6 copy-start
  59.1 2.9 copy-start.2
  59.1 5.4 %copy-start.1 = (bf16[16384,128]{1,0:T(8,128)(2,1)S(1)}, bf16[16384,128]{1,0:T(8,128)(2,1)}, u32[]{:S(2)}) copy-start(bf16[16384,128]{1,0:T(8,128)(2,1)} %gather_fusion) | copy-start | bytes 12582916
  100.5 19.3 %collective-permute-start = (bf16[8,2,256,128]{3,2,1,0:T(8,128)(2,1)S(1)}, bf16[8,2,256,128]{3,2,1,0:T(8,128)(2,1)S(1)}, u32[]{:S(2)}, u32[]{:S(2)}) collective-permute-start(bf16[8,2,256,128]{3,2,1,0:T(8,128)(2,1)S(1)} %bitcast.59), channel_id=1, source_target_pairs={{0,16},{16,0},{32,48},{48,32},{64,80},{80,64},{96,112},{112,96},{1... | collective-permute-start | bytes 3145736 | tf_op jit(solution)/shard_map/ppermute | solution.py:19
  102.5 257.3 %collective-permute-start.1 = (bf16[8,2,256,128]{3,2,1,0:T(8,128)(2,1)S(1)}, bf16[8,2,256,128]{3,2,1,0:T(8,128)(2,1)S(1)}, u32[]{:S(2)}, u32[]{:S(2)}) collective-permute-start(bf16[8,2,256,128]{3,2,1,0:T(8,128)(2,1)S(1)} %bitcast.60), channel_id=1, source_target_pairs={{0,32},{32,0},{16,48},{48,16},{64,96},{96,64},{80,112},{112,80},{1... | collective-permute-start | bytes 3145736 | tf_op jit(solution)/shard_map/ppermute | solution.py:19
  111.6 249.3 %collective-permute-start.3 = (bf16[8,2,256,128]{3,2,1,0:T(8,128)(2,1)S(1)}, bf16[8,2,256,128]{3,2,1,0:T(8,128)(2,1)S(1)}, u32[]{:S(2)}, u32[]{:S(2)}) collective-permute-start(bf16[8,2,256,128]{3,2,1,0:T(8,128)(2,1)S(1)} %bitcast.61), channel_id=1, source_target_pairs={{0,64},{64,0},{16,80},{80,16},{32,96},{96,32},{48,112},{112,48},{1... | collective-permute-start | bytes 3145736 | tf_op jit(solution)/shard_map/ppermute | solution.py:19
  119.8 262.5 %collective-permute-start.2 = (bf16[8,2,256,128]{3,2,1,0:T(8,128)(2,1)S(1)}, bf16[8,2,256,128]{3,2,1,0:T(8,128)(2,1)S(1)}, u32[]{:S(2)}, u32[]{:S(2)}) collective-permute-start(bf16[8,2,256,128]{3,2,1,0:T(8,128)(2,1)S(1)} %collective-permute-done), channel_id=1, source_target_pairs={{0,32},{32,0},{16,48},{48,16},{64,96},{96,64},{80,112},{112,80},{1... | collective-permute-start | bytes 3145736 | tf_op jit(solution)/shard_map/ppermute | solution.py:19
where the time goes:
time: 392 us; the launch traced here: 389 us
  waiting for transfers between devices  255 us (65%)
  local copies, waits for them, and re-layouts  63 us (16%)
  blocking collectives  33.4 us (9%)
  starting transfers between devices  24.7 us (6%)
  other arithmetic  9.15 us (2%)
    ppermute x4, waiting for transfers between devices, partner(): return lax.ppermute(block, axis, route)  255 us
    gather x1, local copies, waits for them, and re-layouts, per_device(): windows = traces[sample_index]  57.4 us
    all_to_all x1, blocking collectives, per_device(): lax.all_to_all(white, 'freq', split_axis=0, concat_axis=2, tiled=True)  33.4 us
    ppermute x4, starting transfers between devices, partner(): return lax.ppermute(block, axis, route)  24.7 us
  transfers between devices with their start and end apart: 4, of which 2 were waited for; matrix products, arithmetic and copies ran while one was open for 1% of the time, Pallas kernels for 0%

commit v1 on v0

v1 whole, which is shorter than its diff:
```python
import math

import jax
import jax.numpy as jnp
from jax import lax
from jax.experimental import pallas as pl
from jax.experimental.pallas import tpu as pltpu
from jax.sharding import PartitionSpec as P

L = 1024
K = 128
WD = 16
SEG = 8704
CB = 128
NF = 16
KL = K // NF
HB = KL // 2
SCALE = 1.0 / math.sqrt(NF * WD)
MIB = 1 << 20

SIN_TERMS = [(-1) ** i * (2.0 * math.pi) ** (2 * i + 1) / math.factorial(2 * i + 1) for i in range(7)]


def table_rows(bins):
    shape = (2 * K, L)
    sample = lax.broadcasted_iota(jnp.int32, shape, 1)
    part = lax.broadcasted_iota(jnp.int32, shape, 0) & 1
    phase = (bins * sample + part * (L // 4)) & (L - 1)
    folded = jnp.minimum(phase, L - phase) - L // 4
    turn = folded.astype(jnp.float32) * (1.0 / L)
    square = turn * turn
    total = jnp.full(shape, SIN_TERMS[-1], jnp.float32)
    for term in SIN_TERMS[-2::-1]:
        total = total * square + term
    return (-(total * turn)).astype(jnp.bfloat16)


def front_kernel(starts, half, bins, taper, traces, near, other, wide, table, tapered, spectra):
    table[...] = table_rows(bins[...])
    wide[...] = traces[...].astype(jnp.float32)
    for pair in range(WD // 2):
        slot = tapered.at[pair % 2]
        for side in range(2):
            first = starts[2 * pair + side]
            mean = jnp.sum(wide[pl.ds(first, L), :], axis=0, keepdims=True) * (1.0 / L)
            slot[:, side * CB : (side + 1) * CB] = ((wide[pl.ds(first, L), :] - mean) * taper[...]).astype(jnp.bfloat16)
        found = jnp.dot(table[...], slot[...], preferred_element_type=jnp.float32)
        for side in range(2):
            spectra[pl.ds(2 * pair + side, 2 * K, stride=WD), :] = found[:, side * CB : (side + 1) * CB]

    rows = 2 * KL * WD

    def add(f, power):
        part = spectra[pl.ds(pl.multiple_of(f * rows, rows), rows), :].reshape(2 * KL, WD, CB)
        return power + jnp.sum(part * part, axis=0)

    power = lax.fori_loop(0, NF, add, jnp.zeros((WD, CB), jnp.float32))
    gain = lax.rsqrt(power * (1.0 / (2 * K)) + 1e-6)[None]

    def whiten(f, carry):
        for out, which in ((near, half[0]), (other, 1 - half[0])):
            start = pl.multiple_of(f * rows + which * (rows // 2), rows // 2)
            part = spectra[pl.ds(start, rows // 2), :].reshape(KL, WD, CB)
            out[f] = (part * gain).astype(jnp.bfloat16).reshape(HB, 2, WD, CB)
        return carry

    lax.fori_loop(0, NF, whiten, 0)


def front(traces, kept_bins, window_starts, half):
    taper = 0.5 - 0.5 * jnp.cos(jnp.arange(L, dtype=jnp.float32) * (2.0 * math.pi / L))
    taper = jnp.broadcast_to(taper[:, None], (L, CB))
    bins = jnp.repeat(kept_bins, 2)[:, None]
    vmem = pl.BlockSpec(memory_space=pltpu.VMEM)
    smem = pl.BlockSpec(memory_space=pltpu.SMEM)
    piece = jax.ShapeDtypeStruct((NF, HB, 2, WD, CB), jnp.bfloat16)
    return pl.pallas_call(
        front_kernel,
        out_shape=(piece, piece),
        in_specs=[smem, smem, vmem, vmem, vmem],
        out_specs=(vmem, vmem),
        scratch_shapes=[
            pltpu.VMEM((SEG, CB), jnp.float32),
            pltpu.VMEM((2 * K, L), jnp.bfloat16),
            pltpu.VMEM((2, L, 2 * CB), jnp.bfloat16),
            pltpu.VMEM((2 * K * WD, CB), jnp.float32),
        ],
        compiler_params=pltpu.CompilerParams(vmem_limit_bytes=40 * MIB),
        name="white",
    )(window_starts, half, bins, taper, traces)


def left_side(ref):
    return jnp.concatenate([ref[:, 0, e].reshape(NF * WD, CB) for e in range(2)], axis=0)


def right_side(ref):
    real, imag = (ref[:, 0, e].reshape(NF * WD, CB) for e in range(2))
    return jnp.concatenate([jnp.concatenate([real, imag], axis=0), jnp.concatenate([-imag, real], axis=0)], axis=1)


def cross(left, right):
    found = lax.dot_general(left, right, (((0,), (0,)), ((), ())), preferred_element_type=jnp.float32)
    return (found * SCALE).astype(jnp.bfloat16)


def rounds_kernel(half, own, own_swapped, far, far_swapped, *rest):
    out = rest[-1]
    left = left_side(own)
    for r, ref in enumerate((own_swapped, far, far_swapped)):
        found = cross(left, right_side(ref))
        for e in range(2):
            out[r, e, 0] = found[:, e * CB : (e + 1) * CB]


def rounds(half, own, own_swapped, far, far_swapped, base=None):
    piece = pl.BlockSpec((NF, 1, 2, WD, CB), lambda k, half: (0, k, 0, 0, 0))
    given = [own, own_swapped, far, far_swapped]
    specs = [piece] * 4
    aliases = {}
    if base is not None:
        given.append(base)
        specs.append(pl.BlockSpec(memory_space=pl.ANY))
        aliases = {5: 0}
    return pl.pallas_call(
        rounds_kernel,
        out_shape=jax.ShapeDtypeStruct((4, 2, KL, CB, CB), jnp.bfloat16),
        grid_spec=pltpu.PrefetchScalarGridSpec(
            num_scalar_prefetch=1,
            grid=(HB,),
            in_specs=specs,
            out_specs=pl.BlockSpec((3, 2, 1, CB, CB), lambda k, half: (0, 0, half[0] * HB + k, 0, 0)),
        ),
        input_output_aliases=aliases,
        compiler_params=pltpu.CompilerParams(vmem_limit_bytes=40 * MIB),
        name="rounds",
    )(half, *given)


def between_kernel(far, side, to_far, to_side):
    for out, a, b in ((to_far, far, side), (to_side, side, far)):
        found = cross(left_side(a), right_side(b))
        for e in range(2):
            out[e, 0] = found[:, e * CB : (e + 1) * CB]


def between(far, side):
    piece = pl.BlockSpec((NF, 1, 2, WD, CB), lambda k: (0, k, 0, 0, 0))
    out = pl.BlockSpec((2, 1, CB, CB), lambda k: (0, k, 0, 0))
    shape = jax.ShapeDtypeStruct((2, HB, CB, CB), jnp.bfloat16)
    return pl.pallas_call(
        between_kernel,
        out_shape=(shape, shape),
        grid=(HB,),
        in_specs=[piece, piece],
        out_specs=(out, out),
        compiler_params=pltpu.CompilerParams(vmem_limit_bytes=40 * MIB),
        name="between",
    )(far, side)


def place_kernel(half, first, second, base, out, sems):
    copies = []
    for ref, which, n in ((first, half[0], 0), (second, 1 - half[0], 1)):
        copies.append(pltpu.make_async_copy(ref, out.at[3, :, pl.ds(which * HB, HB)], sems.at[n]))
    for copy in copies:
        copy.start()
    for copy in copies:
        copy.wait()


def place(half, first, second, base):
    anywhere = pl.BlockSpec(memory_space=pl.ANY)
    return pl.pallas_call(
        place_kernel,
        out_shape=jax.ShapeDtypeStruct(base.shape, base.dtype),
        in_specs=[pl.BlockSpec(memory_space=pltpu.SMEM), anywhere, anywhere, anywhere],
        out_specs=anywhere,
        scratch_shapes=[pltpu.SemaphoreType.DMA((2,))],
        input_output_aliases={3: 0},
        name="place",
    )(half, first, second, base)


def partner(block, mask):
    count = lax.axis_size("chan")
    return lax.ppermute(block, "chan", [(i, i ^ mask) for i in range(count)])


def turn(piece):
    return lax.all_to_all(piece, "freq", split_axis=0, concat_axis=0, tiled=True)


def together(*arrays):
    return lax.optimization_barrier(arrays)


def per_device(traces, kept_bins, window_starts):
    half = ((lax.axis_index("chan") >> 2) & 1).astype(jnp.int32).reshape(1)
    near, other = front(traces, kept_bins, window_starts, half)
    own_near = turn(near)
    far_near = partner(own_near, 2)
    other, _ = together(other, own_near)
    own_other = turn(other)
    side = partner(own_other, 6)
    far_other = partner(own_other, 2)
    far_near, side = together(far_near, side)
    to_far, to_side = between(far_near, side)
    first, second = partner(to_far, 2), partner(to_side, 6)
    base = rounds(half, own_near, partner(own_near, 1), far_near, partner(far_near, 1))
    base = rounds(1 - half, own_other, partner(own_other, 1), far_other, partner(far_other, 1), base)
    return place(half, first, second, base)


def solution(mesh):
    return jax.shard_map(
        per_device,
        mesh=mesh,
        in_specs=(P("freq", "chan"), P(), P("freq")),
        out_specs=P(None, None, "freq", "chan", None),
        check_vma=False,
    )
```

time: 392 us -> 194 us (0.49)
  waiting for transfers between devices: 255 us -> 59 us
  local copies, waits for them, and re-layouts: 63 us -> 3.99 us
  starting transfers between devices: 24.7 us -> 75.1 us
  Pallas kernels: 0 us -> 29.8 us
  blocking collectives: 33.4 us -> 22.1 us
  other arithmetic: 9.15 us -> 0.05 us
    ppermute x4 -> x9, waiting for transfers between devices: 255 us -> 45.8 us  [partner(): return lax.ppermute(block, 'chan', [(i, i ^ mask) for i in range(count)])]
    gather x1 -> x0, local copies, waits for them, and re-layouts: 57.4 us -> none  [per_device(): windows = traces[sample_index]]
    ppermute x4 -> x9, starting transfers between devices: 24.7 us -> 68.7 us  [partner(): return lax.ppermute(block, 'chan', [(i, i ^ mask) for i in range(count)])]
    pallas_call x0 -> x5, Pallas kernels: none -> 29.8 us  [the longest x1 17 us: place(): pl.pallas_call(place_kernel, out_shape=jax.ShapeDtypeStruct(base.shape, b...]
    all_to_all x0 -> x1, waiting for transfers between devices: none -> 13.2 us  [turn(): lax.all_to_all(piece, 'freq', split_axis=0, concat_axis=0, tiled=True)]
    all_to_all x1, blocking collectives: 33.4 us -> 22.1 us  [turn(): lax.all_to_all(piece, 'freq', split_axis=0, concat_axis=0, tiled=True)]
    all_to_all x0 -> x1, starting transfers between devices: none -> 6.38 us  [turn(): lax.all_to_all(piece, 'freq', split_axis=0, concat_axis=0, tiled=True)]
    another operation x2 -> x0, other arithmetic: 4.04 us -> none
  transfers between devices with their start and end apart: 4 -> 10, of which waited for: 2 -> 5; matrix products, arithmetic and copies ran while one was open for 1% -> 0% of each run, Pallas kernels for 0% -> 3%
where the time goes in v1:
time: 194 us; the launch traced here: 190 us
  starting transfers between devices  75.1 us (39%)
  waiting for transfers between devices  59 us (30%)
  Pallas kernels  29.8 us (15%)
  blocking collectives  22.1 us (11%)
  local copies, waits for them, and re-layouts  3.99 us (2%)
    ppermute x9, starting transfers between devices, partner(): return lax.ppermute(block, 'chan', [(i, i ^ mask) for i in range(count)])  68.7 us
    ppermute x9, waiting for transfers between devices, partner(): return lax.ppermute(block, 'chan', [(i, i ^ mask) for i in range(count)])  45.8 us
    all_to_all x1, blocking collectives, turn(): lax.all_to_all(piece, 'freq', split_axis=0, concat_axis=0, tiled=True)  22.1 us
    pallas_call x1, Pallas kernels, place(): pl.pallas_call(place_kernel, out_shape=jax.ShapeDtypeStruct(base.shape, b...  17 us
    all_to_all x1, waiting for transfers between devices, turn(): lax.all_to_all(piece, 'freq', split_axis=0, concat_axis=0, tiled=True)  13.2 us
    pallas_call x1, Pallas kernels, front(): pl.pallas_call(front_kernel, out_shape=(piece, piece), in_specs=[smem, sm...  6.53 us
    all_to_all x1, starting transfers between devices, turn(): lax.all_to_all(piece, 'freq', split_axis=0, concat_axis=0, tiled=True)  6.38 us
    pallas_call x2, Pallas kernels, rounds(): pl.pallas_call(rounds_kernel, out_shape=jax.ShapeDtypeStruct((4, 2, KL, C...  4.96 us
  transfers between devices with their start and end apart: 10, of which 5 were waited for; matrix products, arithmetic and copies ran while one was open for 0% of the time, Pallas kernels for 3%

profile of v1, /device:TPU:6, one launch (start us, length us, event | category | flops | bytes accessed | tf_op | source)
XLA Modules:
  0.0 190.2 jit_solution(11704593857751916544)
XLA Ops:
  0.1 0.7 broadcast_in_dim.4
  0.8 0.1 broadcast_in_dim_reshape.4.bins
  0.9 0.2 broadcast_in_dim.10.taper
  1.1 0.0 copy-start
  1.1 1.6 copy-done
  2.7 0.7 copy-done.1
  3.4 6.5 %white.1 = (bf16[16,4,2,16,128]{4,3,2,1,0:T(8,128)(2,1)S(1)}, bf16[16,4,2,16,128]{4,3,2,1,0:T(8,128)(2,1)}) custom-call(s32[16]{0:T(128)S(1)} %copy-done.1, s32[1]{0:T(128)} %bitcast.half, s32[256,1]{1,0:T(8,128)S(1)} %broadcast_in_dim_reshape.4.bins, f32[1024,128]{1,0:T(8,128)S(1)} %broadcast_in_dim.10.taper, bf16[8704,128]{1,0:T(8,128)(2,1)S(1)} %copy-done), custom_call_target="tpu_custom_call" | custom-call | tf_op jit(solution)/shard_map/white/pallas_call | solution.py:77
  9.9 22.1 %all_to_all.10.own = bf16[16,4,2,16,128]{4,3,2,1,0:T(8,128)(2,1)S(1)} all-to-all(bf16[16,4,2,16,128]{4,3,2,1,0:T(8,128)(2,1)S(1)} %get-tuple-element.12), channel_id=1, replica_groups=mesh['chan'=32,'freq'=16] {'freq'}, dimensions={0} | all-to-all | bytes 1048576 | tf_op jit(solution)/shard_map/all_to_all | solution.py:191
  32.0 6.4 %all-to-all-start.1 = ((bf16[16,4,2,16,128]{4,3,2,1,0:T(8,128)(2,1)}), bf16[16,4,2,16,128]{4,3,2,1,0:T(8,128)(2,1)S(1)}, u32[]{:S(2)}, u32[]{:S(2)}) async-start(bf16[16,4,2,16,128]{4,3,2,1,0:T(8,128)(2,1)} %get-tuple-element.14), calls=%async_computation.1 | async-start | bytes 1048576 | tf_op jit(solution)/shard_map/all_to_all | solution.py:191
  38.4 9.1 %collective-permute-start = (bf16[16,4,2,16,128]{4,3,2,1,0:T(8,128)(2,1)S(1)}, bf16[16,4,2,16,128]{4,3,2,1,0:T(8,128)(2,1)S(1)}, u32[]{:S(2)}, u32[]{:S(2)}) collective-permute-start(bf16[16,4,2,16,128]{4,3,2,1,0:T(8,128)(2,1)S(1)} %all_to_all.10.own), channel_id=1, source_target_pairs={{0,32},{16,48},{32,0},{48,16},{64,96},{80,112},{96,64},{112,80},{1... | collective-permute-start | bytes 1572872 | tf_op jit(solution)/shard_map/ppermute | solution.py:187
  47.5 13.2 %all-to-all-done.1.own = bf16[16,4,2,16,128]{4,3,2,1,0:T(8,128)(2,1)S(1)} async-done(((bf16[16,4,2,16,128]{4,3,2,1,0:T(8,128)(2,1)}), bf16[16,4,2,16,128]{4,3,2,1,0:T(8,128)(2,1)S(1)}, u32[]{:S(2)}, u32[]{:S(2)}) %all-to-all-start.1) | async-done | bytes 524320 | tf_op jit(solution)/shard_map/all_to_all | solution.py:191
  60.7 35.6 %collective-permute-start.1 = (bf16[16,4,2,16,128]{4,3,2,1,0:T(8,128)(2,1)S(1)}, bf16[16,4,2,16,128]{4,3,2,1,0:T(8,128)(2,1)S(1)}, u32[]{:S(2)}, u32[]{:S(2)}) collective-permute-start(bf16[16,4,2,16,128]{4,3,2,1,0:T(8,128)(2,1)S(1)} %all-to-all-done.1.own), channel_id=1, source_target_pairs={{0,96},{16,112},{32,64},{48,80},{64,32},{80,48},{96,0},{112,16},{1... | collective-permute-start | bytes 1572872 | tf_op jit(solution)/shard_map/ppermute | solution.py:187
  96.3 1.9 %collective-permute-start.5 = (bf16[16,4,2,16,128]{4,3,2,1,0:T(8,128)(2,1)S(1)}, bf16[16,4,2,16,128]{4,3,2,1,0:T(8,128)(2,1)S(1)}, u32[]{:S(2)}, u32[]{:S(2)}) collective-permute-start(bf16[16,4,2,16,128]{4,3,2,1,0:T(8,128)(2,1)S(1)} %all-to-all-done.1.own), channel_id=1, source_target_pairs={{0,32},{16,48},{32,0},{48,16},{64,96},{80,112},{96,64},{112,80},{1... | collective-permute-start | bytes 1572872 | tf_op jit(solution)/shard_map/ppermute | solution.py:187
  98.2 1.9 %collective-permute-start.7 = (bf16[16,4,2,16,128]{4,3,2,1,0:T(8,128)(2,1)S(1)}, bf16[16,4,2,16,128]{4,3,2,1,0:T(8,128)(2,1)S(1)}, u32[]{:S(2)}, u32[]{:S(2)}) collective-permute-start(bf16[16,4,2,16,128]{4,3,2,1,0:T(8,128)(2,1)S(1)} %all_to_all.10.own), channel_id=1, source_target_pairs={{0,16},{16,0},{32,48},{48,32},{64,80},{80,64},{96,112},{112,96},{1... | collective-permute-start | bytes 1572872 | tf_op jit(solution)/shard_map/ppermute | solution.py:187
  100.2 0.0 collective-permute-done.far
  100.2 22.4 %collective-permute-done.1.side = bf16[16,4,2,16,128]{4,3,2,1,0:T(8,128)(2,1)S(1)} collective-permute-done((bf16[16,4,2,16,128]{4,3,2,1,0:T(8,128)(2,1)S(1)}, bf16[16,4,2,16,128]{4,3,2,1,0:T(8,128)(2,1)S(1)}, u32[]{:S(2)}, u32[]{:S(2)}) %collective-permute-start.1) | collective-permute-done | bytes 524320 | tf_op jit(solution)/shard_map/ppermute | solution.py:187
  122.6 1.9 %collective-permute-start.8 = (bf16[16,4,2,16,128]{4,3,2,1,0:T(8,128)(2,1)S(1)}, bf16[16,4,2,16,128]{4,3,2,1,0:T(8,128)(2,1)S(1)}, u32[]{:S(2)}, u32[]{:S(2)}) collective-permute-start(bf16[16,4,2,16,128]{4,3,2,1,0:T(8,128)(2,1)S(1)} %collective-permute-done.far), channel_id=1, source_target_pairs={{0,16},{16,0},{32,48},{48,32},{64,80},{80,64},{96,112},{112,96},{1... | collective-permute-start | bytes 1572872 | tf_op jit(solution)/shard_map/ppermute | solution.py:187
  124.5 2.4 %collective-permute-start.4 = (bf16[16,4,2,16,128]{4,3,2,1,0:T(8,128)(2,1)S(1)}, bf16[16,4,2,16,128]{4,3,2,1,0:T(8,128)(2,1)S(1)}, u32[]{:S(2)}, u32[]{:S(2)}) collective-permute-start(bf16[16,4,2,16,128]{4,3,2,1,0:T(8,128)(2,1)S(1)} %all-to-all-done.1.own), channel_id=1, source_target_pairs={{0,16},{16,0},{32,48},{48,32},{64,80},{80,64},{96,112},{112,96},{1... | collective-permute-start | bytes 1572872 | tf_op jit(solution)/shard_map/ppermute | solution.py:187
  126.9 9.8 %collective-permute-done.5.far = bf16[16,4,2,16,128]{4,3,2,1,0:T(8,128)(2,1)S(1)} collective-permute-done((bf16[16,4,2,16,128]{4,3,2,1,0:T(8,128)(2,1)S(1)}, bf16[16,4,2,16,128]{4,3,2,1,0:T(8,128)(2,1)S(1)}, u32[]{:S(2)}, u32[]{:S(2)}) %collective-permute-start.5) | collective-permute-done | bytes 524320 | tf_op jit(solution)/shard_map/ppermute | solution.py:187
  136.7 1.9 %collective-permute-start.6 = (bf16[16,4,2,16,128]{4,3,2,1,0:T(8,128)(2,1)S(1)}, bf16[16,4,2,16,128]{4,3,2,1,0:T(8,128)(2,1)S(1)}, u32[]{:S(2)}, u32[]{:S(2)}) collective-permute-start(bf16[16,4,2,16,128]{4,3,2,1,0:T(8,128)(2,1)S(1)} %collective-permute-done.5.far), channel_id=1, source_target_pairs={{0,16},{16,0},{32,48},{48,32},{64,80},{80,64},{96,112},{112,96},{1... | collective-permute-start | bytes 1572872 | tf_op jit(solution)/shard_map/ppermute | solution.py:187
  138.6 1.3 between.1
  140.0 1.9 %collective-permute-start.2 = (bf16[2,4,128,128]{3,2,1,0:T(8,128)(2,1)S(1)}, bf16[2,4,128,128]{3,2,1,0:T(8,128)(2,1)S(1)}, u32[]{:S(2)}, u32[]{:S(2)}) collective-permute-start(bf16[2,4,128,128]{3,2,1,0:T(8,128)(2,1)S(1)} %get-tuple-element.17), channel_id=1, source_target_pairs={{0,32},{16,48},{32,0},{48,16},{64,96},{80,112},{96,64},{112,80},{1... | collective-permute-start | bytes 786440 | tf_op jit(solution)/shard_map/ppermute | solution.py:187
  141.9 0.0 collective-permute-done.7.own_swapped
  141.9 12.1 %collective-permute-start.3 = (bf16[2,4,128,128]{3,2,1,0:T(8,128)(2,1)S(1)}, bf16[2,4,128,128]{3,2,1,0:T(8,128)(2,1)S(1)}, u32[]{:S(2)}, u32[]{:S(2)}) collective-permute-start(bf16[2,4,128,128]{3,2,1,0:T(8,128)(2,1)S(1)} %get-tuple-element.18), channel_id=1, source_target_pairs={{0,96},{16,112},{32,64},{48,80},{64,32},{80,48},{96,0},{112,16},{1... | collective-permute-start | bytes 786440 | tf_op jit(solution)/shard_map/ppermute | solution.py:187
  154.0 0.0 collective-permute-done.8.far_swapped
  154.0 2.5 %rounds.2.rest_0_ = bf16[4,2,8,128,128]{4,3,2,1,0:T(8,128)(2,1)} custom-call(s32[1]{0:T(128)} %bitcast.half, bf16[16,4,2,16,128]{4,3,2,1,0:T(8,128)(2,1)S(1)} %all_to_all.10.own, bf16[16,4,2,16,128]{4,3,2,1,0:T(8,128)(2,1)S(1)} %collective-permute-done.7.own_swapped, bf16[16,4,2,16,128]{4,3,2,1,0:T(8,128)(2,1)S(1)} %collective-permute-done.far, ...), custom_call_target="tpu_custom_call" | custom-call | tf_op jit(solution)/shard_map/rounds/pallas_call | solution.py:125
  156.5 0.0 collective-permute-done.6.far_swapped
  156.5 2.5 %rounds.3.base = bf16[4,2,8,128,128]{4,3,2,1,0:T(8,128)(2,1)} custom-call(s32[1]{0:T(128)S(6)} %sub.11.half, bf16[16,4,2,16,128]{4,3,2,1,0:T(8,128)(2,1)S(1)} %all-to-all-done.1.own, bf16[16,4,2,16,128]{4,3,2,1,0:T(8,128)(2,1)S(1)} %collective-permute-done.4.own_swapped, ...), custom_call_target="tpu_custom_call", output_to_operand_aliasing={{}: (5, {})} | custom-call | tf_op jit(solution)/shard_map/rounds/pallas_call | solution.py:125
  158.9 4.2 %collective-permute-done.2.first = bf16[2,4,128,128]{3,2,1,0:T(8,128)(2,1)S(1)} collective-permute-done((bf16[2,4,128,128]{3,2,1,0:T(8,128)(2,1)S(1)}, bf16[2,4,128,128]{3,2,1,0:T(8,128)(2,1)S(1)}, u32[]{:S(2)}, u32[]{:S(2)}) %collective-permute-start.2) | collective-permute-done | bytes 262176 | tf_op jit(solution)/shard_map/ppermute | solution.py:187
  163.1 9.4 %collective-permute-done.3.second = bf16[2,4,128,128]{3,2,1,0:T(8,128)(2,1)S(1)} collective-permute-done((bf16[2,4,128,128]{3,2,1,0:T(8,128)(2,1)S(1)}, bf16[2,4,128,128]{3,2,1,0:T(8,128)(2,1)S(1)}, u32[]{:S(2)}, u32[]{:S(2)}) %collective-permute-start.3) | collective-permute-done | bytes 262176 | tf_op jit(solution)/shard_map/ppermute | solution.py:187
  172.5 0.7 copy-done.3
  173.2 17.0 %place.1 = bf16[4,2,8,128,128]{4,3,2,1,0:T(8,128)(2,1)} custom-call(s32[1]{0:T(128)} %bitcast.half, bf16[2,4,128,128]{3,2,1,0:T(8,128)(2,1)} %copy-done.2, bf16[2,4,128,128]{3,2,1,0:T(8,128)(2,1)} %copy-done.3, bf16[4,2,8,128,128]{4,3,2,1,0:T(8,128)(2,1)} %rounds.3.base), custom_call_target="tpu_custom_call", output_to_operand_aliasing={{}: (3, {})} | custom-call | tf_op jit(solution)/shard_map/place/pallas_call | solution.py:174
  (6 shorter events, 0.1 us)
Async XLA Ops:
  1.1 1.6 copy-start
  2.7 0.7 copy-start.1
  32.0 28.7 %all-to-all-start.1 = ((bf16[16,4,2,16,128]{4,3,2,1,0:T(8,128)(2,1)}), bf16[16,4,2,16,128]{4,3,2,1,0:T(8,128)(2,1)S(1)}, u32[]{:S(2)}, u32[]{:S(2)}) async-start(bf16[16,4,2,16,128]{4,3,2,1,0:T(8,128)(2,1)} %get-tuple-element.14), calls=%async_computation.1 | async-start | bytes 1048576 | tf_op jit(solution)/shard_map/all_to_all | solution.py:191
  38.4 61.7 %collective-permute-start = (bf16[16,4,2,16,128]{4,3,2,1,0:T(8,128)(2,1)S(1)}, bf16[16,4,2,16,128]{4,3,2,1,0:T(8,128)(2,1)S(1)}, u32[]{:S(2)}, u32[]{:S(2)}) collective-permute-start(bf16[16,4,2,16,128]{4,3,2,1,0:T(8,128)(2,1)S(1)} %all_to_all.10.own), channel_id=1, source_target_pairs={{0,32},{16,48},{32,0},{48,16},{64,96},{80,112},{96,64},{112,80},{1... | collective-permute-start | bytes 1572872 | tf_op jit(solution)/shard_map/ppermute | solution.py:187
  60.7 61.9 %collective-permute-start.1 = (bf16[16,4,2,16,128]{4,3,2,1,0:T(8,128)(2,1)S(1)}, bf16[16,4,2,16,128]{4,3,2,1,0:T(8,128)(2,1)S(1)}, u32[]{:S(2)}, u32[]{:S(2)}) collective-permute-start(bf16[16,4,2,16,128]{4,3,2,1,0:T(8,128)(2,1)S(1)} %all-to-all-done.1.own), channel_id=1, source_target_pairs={{0,96},{16,112},{32,64},{48,80},{64,32},{80,48},{96,0},{112,16},{1... | collective-permute-start | bytes 1572872 | tf_op jit(solution)/shard_map/ppermute | solution.py:187
  96.3 40.4 %collective-permute-start.5 = (bf16[16,4,2,16,128]{4,3,2,1,0:T(8,128)(2,1)S(1)}, bf16[16,4,2,16,128]{4,3,2,1,0:T(8,128)(2,1)S(1)}, u32[]{:S(2)}, u32[]{:S(2)}) collective-permute-start(bf16[16,4,2,16,128]{4,3,2,1,0:T(8,128)(2,1)S(1)} %all-to-all-done.1.own), channel_id=1, source_target_pairs={{0,32},{16,48},{32,0},{48,16},{64,96},{80,112},{96,64},{112,80},{1... | collective-permute-start | bytes 1572872 | tf_op jit(solution)/shard_map/ppermute | solution.py:187
  98.2 43.7 %collective-permute-start.7 = (bf16[16,4,2,16,128]{4,3,2,1,0:T(8,128)(2,1)S(1)}, bf16[16,4,2,16,128]{4,3,2,1,0:T(8,128)(2,1)S(1)}, u32[]{:S(2)}, u32[]{:S(2)}) collective-permute-start(bf16[16,4,2,16,128]{4,3,2,1,0:T(8,128)(2,1)S(1)} %all_to_all.10.own), channel_id=1, source_target_pairs={{0,16},{16,0},{32,48},{48,32},{64,80},{80,64},{96,112},{112,96},{1... | collective-permute-start | bytes 1572872 | tf_op jit(solution)/shard_map/ppermute | solution.py:187
  122.6 31.4 %collective-permute-start.8 = (bf16[16,4,2,16,128]{4,3,2,1,0:T(8,128)(2,1)S(1)}, bf16[16,4,2,16,128]{4,3,2,1,0:T(8,128)(2,1)S(1)}, u32[]{:S(2)}, u32[]{:S(2)}) collective-permute-start(bf16[16,4,2,16,128]{4,3,2,1,0:T(8,128)(2,1)S(1)} %collective-permute-done.far), channel_id=1, source_target_pairs={{0,16},{16,0},{32,48},{48,32},{64,80},{80,64},{96,112},{112,96},{1... | collective-permute-start | bytes 1572872 | tf_op jit(solution)/shard_map/ppermute | solution.py:187
  124.5 32.0 %collective-permute-start.4 = (bf16[16,4,2,16,128]{4,3,2,1,0:T(8,128)(2,1)S(1)}, bf16[16,4,2,16,128]{4,3,2,1,0:T(8,128)(2,1)S(1)}, u32[]{:S(2)}, u32[]{:S(2)}) collective-permute-start(bf16[16,4,2,16,128]{4,3,2,1,0:T(8,128)(2,1)S(1)} %all-to-all-done.1.own), channel_id=1, source_target_pairs={{0,16},{16,0},{32,48},{48,32},{64,80},{80,64},{96,112},{112,96},{1... | collective-permute-start | bytes 1572872 | tf_op jit(solution)/shard_map/ppermute | solution.py:187
  136.7 19.7 %collective-permute-start.6 = (bf16[16,4,2,16,128]{4,3,2,1,0:T(8,128)(2,1)S(1)}, bf16[16,4,2,16,128]{4,3,2,1,0:T(8,128)(2,1)S(1)}, u32[]{:S(2)}, u32[]{:S(2)}) collective-permute-start(bf16[16,4,2,16,128]{4,3,2,1,0:T(8,128)(2,1)S(1)} %collective-permute-done.5.far), channel_id=1, source_target_pairs={{0,16},{16,0},{32,48},{48,32},{64,80},{80,64},{96,112},{112,96},{1... | collective-permute-start | bytes 1572872 | tf_op jit(solution)/shard_map/ppermute | solution.py:187
  140.0 23.2 %collective-permute-start.2 = (bf16[2,4,128,128]{3,2,1,0:T(8,128)(2,1)S(1)}, bf16[2,4,128,128]{3,2,1,0:T(8,128)(2,1)S(1)}, u32[]{:S(2)}, u32[]{:S(2)}) collective-permute-start(bf16[2,4,128,128]{3,2,1,0:T(8,128)(2,1)S(1)} %get-tuple-element.17), channel_id=1, source_target_pairs={{0,32},{16,48},{32,0},{48,16},{64,96},{80,112},{96,64},{112,80},{1... | collective-permute-start | bytes 786440 | tf_op jit(solution)/shard_map/ppermute | solution.py:187
  141.9 30.6 %collective-permute-start.3 = (bf16[2,4,128,128]{3,2,1,0:T(8,128)(2,1)S(1)}, bf16[2,4,128,128]{3,2,1,0:T(8,128)(2,1)S(1)}, u32[]{:S(2)}, u32[]{:S(2)}) collective-permute-start(bf16[2,4,128,128]{3,2,1,0:T(8,128)(2,1)S(1)} %get-tuple-element.18), channel_id=1, source_target_pairs={{0,96},{16,112},{32,64},{48,80},{64,32},{80,48},{96,0},{112,16},{1... | collective-permute-start | bytes 786440 | tf_op jit(solution)/shard_map/ppermute | solution.py:187
  163.1 9.4 %copy-start.2 = (bf16[2,4,128,128]{3,2,1,0:T(8,128)(2,1)}, bf16[2,4,128,128]{3,2,1,0:T(8,128)(2,1)S(1)}, u32[]{:S(2)}) copy-start(bf16[2,4,128,128]{3,2,1,0:T(8,128)(2,1)S(1)} %collective-permute-done.2.first) | copy-start | bytes 786436
  172.5 0.7 copy-start.3

commit v2 on v1

v2 whole, which is shorter than its diff:
```python
import functools
import math

import jax
import jax.numpy as jnp
from jax import lax
from jax.experimental import pallas as pl
from jax.experimental.pallas import tpu as pltpu
from jax.sharding import PartitionSpec as P

L = 1024
K = 128
WD = 16
SEG = 8704
CB = 128
ROUNDS = 4
NF = 16
KL = K // NF
NX = 4
NZ = 4
HB = KL // 2
SCALE = 1.0 / math.sqrt(NF * WD)
MIB = 1 << 20

SIN_TERMS = [(-1) ** i * (2.0 * math.pi) ** (2 * i + 1) / math.factorial(2 * i + 1) for i in range(7)]


def cosine(phase):
    folded = jnp.minimum(phase, L - phase) - L // 4
    turn = folded.astype(jnp.float32) * (1.0 / L)
    square = turn * turn
    total = jnp.full(phase.shape, SIN_TERMS[-1], jnp.float32)
    for term in SIN_TERMS[-2::-1]:
        total = total * square + term
    return -(total * turn)


def front_kernel(position, starts_in, bins_in, traces, white, *refs):
    crossed, (starts, bins, held, wide, taper, table, tapered, spectra, ready, sems, out_sems) = refs[:NX], refs[NX:]
    copies = [
        pltpu.make_async_copy(bins_in, bins, sems.at[0]),
        pltpu.make_async_copy(starts_in, starts, sems.at[1]),
        pltpu.make_async_copy(traces, held, sems.at[2]),
    ]
    for copy in copies:
        copy.start()
    taper[...] = 0.5 - 0.5 * cosine(lax.broadcasted_iota(jnp.int32, (L, CB), 0))
    copies[0].wait()
    bin_rows = jnp.broadcast_to(bins[...].astype(jnp.float32), (K, K)).T.astype(jnp.int32)
    for block in range(L // K):
        sample = lax.broadcasted_iota(jnp.int32, (K, K), 1) + block * K
        for part in range(2):
            phase = (bin_rows * sample + part * (L // 4)) & (L - 1)
            table[part * K : (part + 1) * K, block * K : (block + 1) * K] = cosine(phase).astype(jnp.bfloat16)
    copies[1].wait()
    copies[2].wait()
    wide[...] = held[...].astype(jnp.float32)
    for pair in range(WD // 2):
        slot = tapered.at[pair % 2]
        for side in range(2):
            first = starts[2 * pair + side]
            mean = jnp.sum(wide[pl.ds(first, L), :], axis=0, keepdims=True) * (1.0 / L)
            slot[:, side * CB : (side + 1) * CB] = ((wide[pl.ds(first, L), :] - mean) * taper[...]).astype(jnp.bfloat16)
        found = jnp.dot(table[...], slot[...], preferred_element_type=jnp.float32)
        for side in range(2):
            for part in range(2):
                first_row = part * WD + 2 * pair + side
                spectra[pl.ds(first_row, K, stride=2 * WD), :] = found[part * K : (part + 1) * K, side * CB : (side + 1) * CB]

    rows = 2 * KL * WD

    def add(f, power):
        part = spectra[pl.ds(pl.multiple_of(f * rows, rows), rows), :].reshape(2 * KL, WD, CB)
        return power + jnp.sum(part * part, axis=0)

    power = lax.fori_loop(0, NF, add, jnp.zeros((WD, CB), jnp.float32))
    gain = lax.rsqrt(power * (1.0 / (2 * K)) + 1e-6)[None]

    def whiten(f, carry):
        for h in range(2):
            first = pl.multiple_of(f * rows + (position[0] ^ h) * (rows // 2), rows // 2)
            part = spectra[pl.ds(first, rows // 2), :].reshape(KL, WD, CB)
            ready[f, h * HB : (h + 1) * HB] = (part * gain).astype(jnp.bfloat16).reshape(HB, 2, WD, CB)
        for number in range(2):
            pltpu.make_async_copy(ready.at[f], white.at[number, f], out_sems.at[number]).start()
        return carry

    lax.fori_loop(0, NF, whiten, 0)
    for e, out in enumerate(crossed):
        for d in range(NZ):
            out[d] = ready[(d * NX + e) ^ position[1], HB:]
    for number in range(2):
        pltpu.make_async_copy(ready, white.at[number], out_sems.at[number]).wait()


def front(traces, kept_bins, window_starts, position):
    vmem = pl.BlockSpec(memory_space=pltpu.VMEM)
    smem = pl.BlockSpec(memory_space=pltpu.SMEM)
    hbm = pl.BlockSpec(memory_space=pltpu.HBM)
    given = [window_starts, kept_bins.reshape(1, K), traces]
    given = [pltpu.with_memory_space_constraint(array, pltpu.HBM) for array in given]
    return pl.pallas_call(
        front_kernel,
        out_shape=(pltpu.HBM((2, NF, KL, 2, WD, CB), jnp.bfloat16),)
        + (jax.ShapeDtypeStruct((NZ, HB, 2, WD, CB), jnp.bfloat16),) * NX,
        in_specs=[smem, hbm, hbm, hbm],
        out_specs=(hbm,) + (vmem,) * NX,
        scratch_shapes=[
            pltpu.SMEM((WD,), jnp.int32),
            pltpu.VMEM((1, K), jnp.int32),
            pltpu.VMEM((SEG, CB), jnp.bfloat16),
            pltpu.VMEM((SEG, CB), jnp.float32),
            pltpu.VMEM((L, CB), jnp.float32),
            pltpu.VMEM((2 * K, L), jnp.bfloat16),
            pltpu.VMEM((2, L, 2 * CB), jnp.bfloat16),
            pltpu.VMEM((2 * K * WD, CB), jnp.float32),
            pltpu.VMEM((NF, KL, 2, WD, CB), jnp.bfloat16),
            pltpu.SemaphoreType.DMA((3,)),
            pltpu.SemaphoreType.DMA((2,)),
        ],
        compiler_params=pltpu.CompilerParams(vmem_limit_bytes=40 * MIB),
        name="white",
    )(position, *given)


def left_side(refs):
    return jnp.concatenate([part_of(refs, 0), part_of(refs, 1)], axis=0)


def part_of(refs, e):
    parts = [ref[..., e, :, :].reshape(-1, CB) for ref in refs]
    return parts[0] if len(parts) == 1 else jnp.concatenate(parts, axis=0)


def right_side(refs):
    real, imag = part_of(refs, 0), part_of(refs, 1)
    return jnp.concatenate([jnp.concatenate([real, imag], axis=0), jnp.concatenate([-imag, real], axis=0)], axis=1)


def cross(left, right):
    found = lax.dot_general(left, right, (((0,), (0,)), ((), ())), preferred_element_type=jnp.float32)
    return (found * SCALE).astype(jnp.bfloat16)


def rounds_kernel(position, own, far, own_swapped, far_swapped, out):
    left = left_side([own])
    for r, ref in enumerate((own_swapped, far, far_swapped)):
        found = cross(left, right_side([ref]))
        for e in range(2):
            out[r, e, 0] = found[:, e * CB : (e + 1) * CB]


def rounds(position, both, both_swapped):
    own = pl.BlockSpec((1, NF, 1, 2, WD, CB), lambda k, position: (position[2], 0, k, 0, 0, 0))
    far = pl.BlockSpec((1, NF, 1, 2, WD, CB), lambda k, position: (1 - position[2], 0, k, 0, 0, 0))
    return pl.pallas_call(
        rounds_kernel,
        out_shape=jax.ShapeDtypeStruct((ROUNDS, 2, KL, CB, CB), jnp.bfloat16),
        grid_spec=pltpu.PrefetchScalarGridSpec(
            num_scalar_prefetch=1,
            grid=(KL,),
            in_specs=[own, far, own, far],
            out_specs=pl.BlockSpec((3, 2, 1, CB, CB), lambda k, position: (0, 0, k ^ (position[0] * HB), 0, 0)),
        ),
        compiler_params=pltpu.CompilerParams(vmem_limit_bytes=40 * MIB),
        name="rounds",
    )(position, both, both, both_swapped, both_swapped)


def between_kernel(position, *refs):
    far, side, (to_far, to_side) = refs[:NF], refs[NF : NF + NZ], refs[NF + NZ :]
    for out, a, b in ((to_far, far, side), (to_side, side, far)):
        found = cross(left_side(a), right_side(b))
        for e in range(2):
            out[e, 0] = found[:, e * CB : (e + 1) * CB]


def between(position, both, side):
    far = [
        pl.BlockSpec((1, 1, 1, 2, WD, CB), lambda k, position, g=g: (1 - position[2], g ^ position[1], k, 0, 0, 0))
        for g in range(NF)
    ]
    piece = pl.BlockSpec((NX, 1, 2, WD, CB), lambda k, position: (0, k, 0, 0, 0))
    out = pl.BlockSpec((2, 1, CB, CB), lambda k, position: (0, k, 0, 0))
    shape = jax.ShapeDtypeStruct((2, HB, CB, CB), jnp.bfloat16)
    return pl.pallas_call(
        between_kernel,
        out_shape=(shape, shape),
        grid_spec=pltpu.PrefetchScalarGridSpec(
            num_scalar_prefetch=1, grid=(HB,), in_specs=far + [piece] * NZ, out_specs=(out, out)
        ),
        compiler_params=pltpu.CompilerParams(vmem_limit_bytes=40 * MIB),
        name="between",
    )(position, *[both] * NF, *side)


def place_kernel(position, first, second, base, out):
    @pl.when(pl.program_id(0) == 0)
    def _():
        out[0] = first[...]

    @pl.when(pl.program_id(0) == 1)
    def _():
        out[0] = second[...]


def place(position, first, second, base):
    whole = pl.BlockSpec((2, HB, CB, CB), lambda step, half: (0, 0, 0, 0))
    return pl.pallas_call(
        place_kernel,
        out_shape=jax.ShapeDtypeStruct(base.shape, base.dtype),
        grid_spec=pltpu.PrefetchScalarGridSpec(
            num_scalar_prefetch=1,
            grid=(2,),
            in_specs=[whole, whole, pl.BlockSpec(memory_space=pl.ANY)],
            out_specs=pl.BlockSpec((1, 2, HB, CB, CB), lambda step, position: (3, 0, position[0] ^ step, 0, 0)),
        ),
        input_output_aliases={3: 0},
        compiler_params=pltpu.CompilerParams(vmem_limit_bytes=40 * MIB),
        name="place",
    )(position, first, second, base)


def partner(block, mask):
    count = lax.axis_size("chan")
    return lax.ppermute(block, "chan", [(i, i ^ mask) for i in range(count)])


def send(block, chan_mask, freq_mask):
    moves = []
    for c in range(lax.axis_size("chan")):
        for f in range(NF):
            moves.append((c * NF + f, (c ^ chan_mask) * NF + (f ^ freq_mask)))
    return lax.ppermute(block, ("chan", "freq"), moves)


def together(*arrays):
    return lax.optimization_barrier(arrays)


def pair_groups(mask):
    pairs = [(c, c ^ mask) for c in range(lax.axis_size("chan")) if c < c ^ mask]
    return [[c * NF + f for c in pair for f in range(NF)] for pair in pairs]


def per_device(traces, kept_bins, window_starts):
    chan, freq = lax.axis_index("chan"), lax.axis_index("freq")
    position = jnp.stack([(chan >> 2) & 1, freq, (chan >> 1) & 1]).astype(jnp.int32)
    white, *crossed = front(traces, kept_bins, window_starts, position)
    crossed = [crossed[0]] + [send(crossed[e], 0, e) for e in range(1, NX)]
    crossed = [jnp.stack([piece[d] for piece in crossed]) for d in range(NZ)]
    side = [send(crossed[d], 6, d * NX) for d in range(NZ)]
    both = lax.all_to_all(
        white.reshape((2 * NF,) + white.shape[2:]),
        ("chan", "freq"),
        split_axis=0,
        concat_axis=0,
        tiled=True,
        axis_index_groups=pair_groups(2),
    ).reshape(white.shape)
    both, *side = together(both, *side)
    to_far, to_side = between(position, both, side)
    first, second = partner(to_far, 2), partner(to_side, 6)
    base = rounds(position, both, partner(both, 1))
    return place(position, first, second, base)


def solution(mesh):
    return jax.shard_map(
        per_device,
        mesh=mesh,
        in_specs=(P("freq", "chan"), P(), P("freq")),
        out_specs=P(None, None, "freq", "chan", None),
        check_vma=False,
    )
```

time: 194 us -> 164 us (0.85); the launches traced: 190 us -> 164 us
  waiting for transfers between devices: 59 us -> 84.9 us
  blocking collectives: 22.1 us -> 0 us
  Pallas kernels: 29.8 us -> 16.6 us
  starting transfers between devices: 75.1 us -> 61.9 us
  local copies, waits for them, and re-layouts: 3.99 us -> 0.04 us
    ppermute x9 -> x3, starting transfers between devices: 68.7 us -> 13.9 us  [partner(): return lax.ppermute(block, 'chan', [(i, i ^ mask) for i in range(count)])]
    ppermute x0 -> x7, waiting for transfers between devices: none -> 52.7 us  [send(): return lax.ppermute(block, ('chan', 'freq'), moves)]
    ppermute x0 -> x7, starting transfers between devices: none -> 32.3 us  [send(): return lax.ppermute(block, ('chan', 'freq'), moves)]
    ppermute x9 -> x3, waiting for transfers between devices: 45.8 us -> 19.2 us  [partner(): return lax.ppermute(block, 'chan', [(i, i ^ mask) for i in range(count)])]
    all_to_all x1 -> x0, blocking collectives: 22.1 us -> none  [turn(): lax.all_to_all(piece, 'freq', split_axis=0, concat_axis=0, tiled=True)]
    pallas_call x1, Pallas kernels: 17 us -> 1.38 us  [place(): pl.pallas_call(place_kernel, out_shape=jax.ShapeDtypeStruct(base.shape, b...]
    all_to_all x1, starting transfers between devices: 6.38 us -> 15.7 us  [per_device(): lax.all_to_all(white.reshape((2 * NF,) + white.shape[2:]), ('chan', 'freq...]
    unnamed x8 -> x0, local copies, waits for them, and re-layouts: 2.98 us -> none
  transfers between devices with their start and end apart: 10 -> 11, of which waited for: 5 -> 7; matrix products, arithmetic and copies ran while one was open for 0% -> 0% of each run, Pallas kernels for 3% -> 4%
where the time goes in v2:
time: 164 us
  waiting for transfers between devices  84.9 us (52%)
  starting transfers between devices  61.9 us (38%)
  Pallas kernels  16.6 us (10%)
    ppermute x7, waiting for transfers between devices, send(): return lax.ppermute(block, ('chan', 'freq'), moves)  52.7 us
    ppermute x7, starting transfers between devices, send(): return lax.ppermute(block, ('chan', 'freq'), moves)  32.3 us
    ppermute x3, waiting for transfers between devices, partner(): return lax.ppermute(block, 'chan', [(i, i ^ mask) for i in range(count)])  19.2 us
    all_to_all x1, starting transfers between devices, per_device(): lax.all_to_all(white.reshape((2 * NF,) + white.shape[2:]), ('chan', 'freq...  15.7 us
    ppermute x3, starting transfers between devices, partner(): return lax.ppermute(block, 'chan', [(i, i ^ mask) for i in range(count)])  13.9 us
    all_to_all x1, waiting for transfers between devices, per_device(): lax.all_to_all(white.reshape((2 * NF,) + white.shape[2:]), ('chan', 'freq...  13 us
    pallas_call x1, Pallas kernels, front(): pl.pallas_call(front_kernel, out_shape=(pltpu.HBM((2, NF, KL, 2, WD, CB),...  8.06 us
    pallas_call x1, Pallas kernels, rounds(): pl.pallas_call(rounds_kernel, out_shape=jax.ShapeDtypeStruct((ROUNDS, 2,...  5.2 us
  transfers between devices with their start and end apart: 11, of which 7 were waited for; matrix products, arithmetic and copies ran while one was open for 0% of the time, Pallas kernels for 4%

profile of v2, /device:TPU:6, one launch (start us, length us, event | category | flops | bytes accessed | tf_op | source)
XLA Modules:
  0.0 163.8 jit_solution(18242952493649607477)
XLA Ops:
  0.0 0.1 pad_add_fusion.position
  0.1 8.1 %white.1 = (bf16[2,16,8,2,16,128]{5,4,3,2,1,0:T(8,128)(2,1)}, bf16[4,4,2,16,128]{4,3,2,1,0:T(8,128)(2,1)S(1)}, bf16[4,4,2,16,128]{4,3,2,1,0:T(8,128)(2,1)S(1)}, ...) custom-call(s32[3]{0:T(128)S(1)} %pad_add_fusion.position, s32[16]{0:T(128)} %starts_in.1, ...), custom_call_target="tpu_custom_call" | custom-call | tf_op jit(solution)/shard_map/white/pallas_call | solution.py:102
  8.1 15.7 %all-to-all-start = ((bf16[32,8,2,16,128]{4,3,2,1,0:T(8,128)(2,1)}), bf16[32,8,2,16,128]{4,3,2,1,0:T(8,128)(2,1)S(1)}, u32[]{:S(2)}, u32[]{:S(2)}) async-start(bf16[32,8,2,16,128]{4,3,2,1,0:T(8,128)(2,1)} %bitcast.25), calls=%async_computation | async-start | bytes 4194304 | tf_op jit(solution)/shard_map/all_to_all | solution.py:253
  23.8 2.8 %collective-permute-start = (bf16[4,4,2,16,128]{4,3,2,1,0:T(8,128)(2,1)S(1)}, bf16[4,4,2,16,128]{4,3,2,1,0:T(8,128)(2,1)S(1)}, u32[]{:S(2)}, u32[]{:S(2)}) collective-permute-start(bf16[4,4,2,16,128]{4,3,2,1,0:T(8,128)(2,1)S(1)} %get-tuple-element.19), channel_id=1, source_target_pairs={{0,1},{1,0},{2,3},{3,2},{4,5},{5,4},{6,7},{7,6},{8,9},{9,8},{10,11... | collective-permute-start | bytes 393224 | tf_op jit(solution)/shard_map/ppermute | solution.py:234
  26.6 2.7 %collective-permute-start.1 = (bf16[4,4,2,16,128]{4,3,2,1,0:T(8,128)(2,1)S(1)}, bf16[4,4,2,16,128]{4,3,2,1,0:T(8,128)(2,1)S(1)}, u32[]{:S(2)}, u32[]{:S(2)}) collective-permute-start(bf16[4,4,2,16,128]{4,3,2,1,0:T(8,128)(2,1)S(1)} %get-tuple-element.20), channel_id=1, source_target_pairs={{0,2},{1,3},{2,0},{3,1},{4,6},{5,7},{6,4},{7,5},{8,10},{9,11},{10,... | collective-permute-start | bytes 393224 | tf_op jit(solution)/shard_map/ppermute | solution.py:234
  29.3 4.9 %collective-permute-start.2 = (bf16[4,4,2,16,128]{4,3,2,1,0:T(8,128)(2,1)S(1)}, bf16[4,4,2,16,128]{4,3,2,1,0:T(8,128)(2,1)S(1)}, u32[]{:S(2)}, u32[]{:S(2)}) collective-permute-start(bf16[4,4,2,16,128]{4,3,2,1,0:T(8,128)(2,1)S(1)} %get-tuple-element.21), channel_id=1, source_target_pairs={{0,3},{1,2},{2,1},{3,0},{4,7},{5,6},{6,5},{7,4},{8,11},{9,10},{10,... | collective-permute-start | bytes 393224 | tf_op jit(solution)/shard_map/ppermute | solution.py:234
  34.3 1.9 %collective-permute-done = bf16[4,4,2,16,128]{4,3,2,1,0:T(8,128)(2,1)S(1)} collective-permute-done((bf16[4,4,2,16,128]{4,3,2,1,0:T(8,128)(2,1)S(1)}, bf16[4,4,2,16,128]{4,3,2,1,0:T(8,128)(2,1)S(1)}, u32[]{:S(2)}, u32[]{:S(2)}) %collective-permute-start) | collective-permute-done | bytes 131104 | tf_op jit(solution)/shard_map/ppermute | solution.py:234
  36.2 4.2 %collective-permute-done.1 = bf16[4,4,2,16,128]{4,3,2,1,0:T(8,128)(2,1)S(1)} collective-permute-done((bf16[4,4,2,16,128]{4,3,2,1,0:T(8,128)(2,1)S(1)}, bf16[4,4,2,16,128]{4,3,2,1,0:T(8,128)(2,1)S(1)}, u32[]{:S(2)}, u32[]{:S(2)}) %collective-permute-start.1) | collective-permute-done | bytes 131104 | tf_op jit(solution)/shard_map/ppermute | solution.py:234
  40.5 2.6 %collective-permute-done.2 = bf16[4,4,2,16,128]{4,3,2,1,0:T(8,128)(2,1)S(1)} collective-permute-done((bf16[4,4,2,16,128]{4,3,2,1,0:T(8,128)(2,1)S(1)}, bf16[4,4,2,16,128]{4,3,2,1,0:T(8,128)(2,1)S(1)}, u32[]{:S(2)}, u32[]{:S(2)}) %collective-permute-start.2) | collective-permute-done | bytes 131104 | tf_op jit(solution)/shard_map/ppermute | solution.py:234
  43.1 5.7 %collective-permute-start.3 = (bf16[4,4,2,16,128]{4,3,2,1,0:T(8,128)(2,1)S(1)}, bf16[4,4,2,16,128]{4,3,2,1,0:T(8,128)(2,1)S(1)}, u32[]{:S(2)}, u32[]{:S(2)}) collective-permute-start(bf16[4,4,2,16,128]{4,3,2,1,0:T(8,128)(2,1)S(1)} %pad_maximum_fusion), channel_id=1, source_target_pairs={{0,96},{1,97},{2,98},{3,99},{4,100},{5,101},{6,102},{7,103},{8,104... | collective-permute-start | bytes 393224 | tf_op jit(solution)/shard_map/ppermute | solution.py:234
  48.9 3.5 %collective-permute-start.4 = (bf16[4,4,2,16,128]{4,3,2,1,0:T(8,128)(2,1)S(1)}, bf16[4,4,2,16,128]{4,3,2,1,0:T(8,128)(2,1)S(1)}, u32[]{:S(2)}, u32[]{:S(2)}) collective-permute-start(bf16[4,4,2,16,128]{4,3,2,1,0:T(8,128)(2,1)S(1)} %pad_maximum_fusion.1), channel_id=1, source_target_pairs={{0,100},{1,101},{2,102},{3,103},{4,96},{5,97},{6,98},{7,99},{8,108... | collective-permute-start | bytes 393224 | tf_op jit(solution)/shard_map/ppermute | solution.py:234
  52.4 10.8 %collective-permute-start.5 = (bf16[4,4,2,16,128]{4,3,2,1,0:T(8,128)(2,1)S(1)}, bf16[4,4,2,16,128]{4,3,2,1,0:T(8,128)(2,1)S(1)}, u32[]{:S(2)}, u32[]{:S(2)}) collective-permute-start(bf16[4,4,2,16,128]{4,3,2,1,0:T(8,128)(2,1)S(1)} %pad_maximum_fusion.2), channel_id=1, source_target_pairs={{0,104},{1,105},{2,106},{3,107},{4,108},{5,109},{6,110},{7,111},{8... | collective-permute-start | bytes 393224 | tf_op jit(solution)/shard_map/ppermute | solution.py:234
  63.2 1.9 %collective-permute-start.6 = (bf16[4,4,2,16,128]{4,3,2,1,0:T(8,128)(2,1)S(1)}, bf16[4,4,2,16,128]{4,3,2,1,0:T(8,128)(2,1)S(1)}, u32[]{:S(2)}, u32[]{:S(2)}) collective-permute-start(bf16[4,4,2,16,128]{4,3,2,1,0:T(8,128)(2,1)S(1)} %pad_maximum_fusion.3), channel_id=1, source_target_pairs={{0,108},{1,109},{2,110},{3,111},{4,104},{5,105},{6,106},{7,107},{8... | collective-permute-start | bytes 393224 | tf_op jit(solution)/shard_map/ppermute | solution.py:234
  65.2 43.9 %collective-permute-done.3.refs_16_ = bf16[4,4,2,16,128]{4,3,2,1,0:T(8,128)(2,1)S(1)} collective-permute-done((bf16[4,4,2,16,128]{4,3,2,1,0:T(8,128)(2,1)S(1)}, bf16[4,4,2,16,128]{4,3,2,1,0:T(8,128)(2,1)S(1)}, u32[]{:S(2)}, u32[]{:S(2)}) %collective-permute-start.3) | collective-permute-done | bytes 131104 | tf_op jit(solution)/shard_map/ppermute | solution.py:234
  109.0 0.0 collective-permute-done.4.refs_17_
  109.0 0.0 collective-permute-done.5.refs_18_
  109.0 0.0 collective-permute-done.6.refs_19_
  109.0 13.0 %all-to-all-done = bf16[32,8,2,16,128]{4,3,2,1,0:T(8,128)(2,1)S(1)} async-done(((bf16[32,8,2,16,128]{4,3,2,1,0:T(8,128)(2,1)}), bf16[32,8,2,16,128]{4,3,2,1,0:T(8,128)(2,1)S(1)}, u32[]{:S(2)}, u32[]{:S(2)}) %all-to-all-start) | async-done | bytes 2097184 | tf_op jit(solution)/shard_map/all_to_all | solution.py:253
  122.0 1.9 %collective-permute-start.9 = (bf16[2,16,8,2,16,128]{5,4,3,2,1,0:T(8,128)(2,1)S(1)}, bf16[2,16,8,2,16,128]{5,4,3,2,1,0:T(8,128)(2,1)S(1)}, u32[]{:S(2)}, u32[]{:S(2)}) collective-permute-start(bf16[2,16,8,2,16,128]{5,4,3,2,1,0:T(8,128)(2,1)S(1)} %bitcast.6), channel_id=1, source_target_pairs={{0,16},{16,0},{32,48},{48,32},{64,80},{80,64},{96,112},{112,96},{1... | collective-permute-start | bytes 6291464 | tf_op jit(solution)/shard_map/ppermute | solution.py:226
  124.0 2.0 %between.1 = (bf16[2,4,128,128]{3,2,1,0:T(8,128)(2,1)S(1)}, bf16[2,4,128,128]{3,2,1,0:T(8,128)(2,1)S(1)}) custom-call(s32[3]{0:T(128)S(1)} %pad_add_fusion.position, bf16[2,16,8,2,16,128]{5,4,3,2,1,0:T(8,128)(2,1)S(1)} %bitcast.7, bf16[2,16,8,2,16,128]{5,4,3,2,1,0:T(8,128)(2,1)S(1)} %bitcast.8, bf16[2,16,8,2,16,128]{5,4,3,2,1,0:T(8,128)(2,1)S(1)} %bitcast.9, ...), custom_call_target="tpu_custom_call" | custom-call | tf_op jit(solution)/shard_map/between/pallas_call | solution.py:186
  126.0 7.7 %collective-permute-start.7 = (bf16[2,4,128,128]{3,2,1,0:T(8,128)(2,1)S(1)}, bf16[2,4,128,128]{3,2,1,0:T(8,128)(2,1)S(1)}, u32[]{:S(2)}, u32[]{:S(2)}) collective-permute-start(bf16[2,4,128,128]{3,2,1,0:T(8,128)(2,1)S(1)} %get-tuple-element.27), channel_id=1, source_target_pairs={{0,32},{16,48},{32,0},{48,16},{64,96},{80,112},{96,64},{112,80},{1... | collective-permute-start | bytes 786440 | tf_op jit(solution)/shard_map/ppermute | solution.py:226
  133.7 4.3 %collective-permute-start.8 = (bf16[2,4,128,128]{3,2,1,0:T(8,128)(2,1)S(1)}, bf16[2,4,128,128]{3,2,1,0:T(8,128)(2,1)S(1)}, u32[]{:S(2)}, u32[]{:S(2)}) collective-permute-start(bf16[2,4,128,128]{3,2,1,0:T(8,128)(2,1)S(1)} %get-tuple-element.28), channel_id=1, source_target_pairs={{0,96},{16,112},{32,64},{48,80},{64,32},{80,48},{96,0},{112,16},{1... | collective-permute-start | bytes 786440 | tf_op jit(solution)/shard_map/ppermute | solution.py:226
  138.0 0.0 collective-permute-done.9.own_swapped.far_swapped
  138.0 5.2 %rounds.1.base = bf16[4,2,8,128,128]{4,3,2,1,0:T(8,128)(2,1)} custom-call(s32[3]{0:T(128)S(1)} %pad_add_fusion.position, bf16[2,16,8,2,16,128]{5,4,3,2,1,0:T(8,128)(2,1)S(1)} %bitcast.23, bf16[2,16,8,2,16,128]{5,4,3,2,1,0:T(8,128)(2,1)S(1)} %bitcast.24, bf16[2,16,8,2,16,128]{5,4,3,2,1,0:T(8,128)(2,1)S(1)} %collective-permute-done.9.own_swapped.far_swapped, ...), custom_call_target="tpu_custom_call" | custom-call | tf_op jit(solution)/shard_map/rounds/pallas_call | solution.py:156
  143.2 8.5 %collective-permute-done.7.first = bf16[2,4,128,128]{3,2,1,0:T(8,128)(2,1)S(1)} collective-permute-done((bf16[2,4,128,128]{3,2,1,0:T(8,128)(2,1)S(1)}, bf16[2,4,128,128]{3,2,1,0:T(8,128)(2,1)S(1)}, u32[]{:S(2)}, u32[]{:S(2)}) %collective-permute-start.7) | collective-permute-done | bytes 262176 | tf_op jit(solution)/shard_map/ppermute | solution.py:226
  151.7 10.7 %collective-permute-done.8.second = bf16[2,4,128,128]{3,2,1,0:T(8,128)(2,1)S(1)} collective-permute-done((bf16[2,4,128,128]{3,2,1,0:T(8,128)(2,1)S(1)}, bf16[2,4,128,128]{3,2,1,0:T(8,128)(2,1)S(1)}, u32[]{:S(2)}, u32[]{:S(2)}) %collective-permute-start.8) | collective-permute-done | bytes 262176 | tf_op jit(solution)/shard_map/ppermute | solution.py:226
  162.4 1.4 place.1
  (8 shorter events, 0.1 us)
Async XLA Ops:
  8.1 113.9 %all-to-all-start = ((bf16[32,8,2,16,128]{4,3,2,1,0:T(8,128)(2,1)}), bf16[32,8,2,16,128]{4,3,2,1,0:T(8,128)(2,1)S(1)}, u32[]{:S(2)}, u32[]{:S(2)}) async-start(bf16[32,8,2,16,128]{4,3,2,1,0:T(8,128)(2,1)} %bitcast.25), calls=%async_computation | async-start | bytes 4194304 | tf_op jit(solution)/shard_map/all_to_all | solution.py:253
  23.8 12.4 %collective-permute-start = (bf16[4,4,2,16,128]{4,3,2,1,0:T(8,128)(2,1)S(1)}, bf16[4,4,2,16,128]{4,3,2,1,0:T(8,128)(2,1)S(1)}, u32[]{:S(2)}, u32[]{:S(2)}) collective-permute-start(bf16[4,4,2,16,128]{4,3,2,1,0:T(8,128)(2,1)S(1)} %get-tuple-element.19), channel_id=1, source_target_pairs={{0,1},{1,0},{2,3},{3,2},{4,5},{5,4},{6,7},{7,6},{8,9},{9,8},{10,11... | collective-permute-start | bytes 393224 | tf_op jit(solution)/shard_map/ppermute | solution.py:234
  26.6 13.9 %collective-permute-start.1 = (bf16[4,4,2,16,128]{4,3,2,1,0:T(8,128)(2,1)S(1)}, bf16[4,4,2,16,128]{4,3,2,1,0:T(8,128)(2,1)S(1)}, u32[]{:S(2)}, u32[]{:S(2)}) collective-permute-start(bf16[4,4,2,16,128]{4,3,2,1,0:T(8,128)(2,1)S(1)} %get-tuple-element.20), channel_id=1, source_target_pairs={{0,2},{1,3},{2,0},{3,1},{4,6},{5,7},{6,4},{7,5},{8,10},{9,11},{10,... | collective-permute-start | bytes 393224 | tf_op jit(solution)/shard_map/ppermute | solution.py:234
  29.3 13.7 %collective-permute-start.2 = (bf16[4,4,2,16,128]{4,3,2,1,0:T(8,128)(2,1)S(1)}, bf16[4,4,2,16,128]{4,3,2,1,0:T(8,128)(2,1)S(1)}, u32[]{:S(2)}, u32[]{:S(2)}) collective-permute-start(bf16[4,4,2,16,128]{4,3,2,1,0:T(8,128)(2,1)S(1)} %get-tuple-element.21), channel_id=1, source_target_pairs={{0,3},{1,2},{2,1},{3,0},{4,7},{5,6},{6,5},{7,4},{8,11},{9,10},{10,... | collective-permute-start | bytes 393224 | tf_op jit(solution)/shard_map/ppermute | solution.py:234
  43.1 65.9 %collective-permute-start.3 = (bf16[4,4,2,16,128]{4,3,2,1,0:T(8,128)(2,1)S(1)}, bf16[4,4,2,16,128]{4,3,2,1,0:T(8,128)(2,1)S(1)}, u32[]{:S(2)}, u32[]{:S(2)}) collective-permute-start(bf16[4,4,2,16,128]{4,3,2,1,0:T(8,128)(2,1)S(1)} %pad_maximum_fusion), channel_id=1, source_target_pairs={{0,96},{1,97},{2,98},{3,99},{4,100},{5,101},{6,102},{7,103},{8,104... | collective-permute-start | bytes 393224 | tf_op jit(solution)/shard_map/ppermute | solution.py:234
  48.9 60.1 %collective-permute-start.4 = (bf16[4,4,2,16,128]{4,3,2,1,0:T(8,128)(2,1)S(1)}, bf16[4,4,2,16,128]{4,3,2,1,0:T(8,128)(2,1)S(1)}, u32[]{:S(2)}, u32[]{:S(2)}) collective-permute-start(bf16[4,4,2,16,128]{4,3,2,1,0:T(8,128)(2,1)S(1)} %pad_maximum_fusion.1), channel_id=1, source_target_pairs={{0,100},{1,101},{2,102},{3,103},{4,96},{5,97},{6,98},{7,99},{8,108... | collective-permute-start | bytes 393224 | tf_op jit(solution)/shard_map/ppermute | solution.py:234
  52.4 56.6 %collective-permute-start.5 = (bf16[4,4,2,16,128]{4,3,2,1,0:T(8,128)(2,1)S(1)}, bf16[4,4,2,16,128]{4,3,2,1,0:T(8,128)(2,1)S(1)}, u32[]{:S(2)}, u32[]{:S(2)}) collective-permute-start(bf16[4,4,2,16,128]{4,3,2,1,0:T(8,128)(2,1)S(1)} %pad_maximum_fusion.2), channel_id=1, source_target_pairs={{0,104},{1,105},{2,106},{3,107},{4,108},{5,109},{6,110},{7,111},{8... | collective-permute-start | bytes 393224 | tf_op jit(solution)/shard_map/ppermute | solution.py:234
  63.2 45.8 %collective-permute-start.6 = (bf16[4,4,2,16,128]{4,3,2,1,0:T(8,128)(2,1)S(1)}, bf16[4,4,2,16,128]{4,3,2,1,0:T(8,128)(2,1)S(1)}, u32[]{:S(2)}, u32[]{:S(2)}) collective-permute-start(bf16[4,4,2,16,128]{4,3,2,1,0:T(8,128)(2,1)S(1)} %pad_maximum_fusion.3), channel_id=1, source_target_pairs={{0,108},{1,109},{2,110},{3,111},{4,104},{5,105},{6,106},{7,107},{8... | collective-permute-start | bytes 393224 | tf_op jit(solution)/shard_map/ppermute | solution.py:234
  122.0 16.0 %collective-permute-start.9 = (bf16[2,16,8,2,16,128]{5,4,3,2,1,0:T(8,128)(2,1)S(1)}, bf16[2,16,8,2,16,128]{5,4,3,2,1,0:T(8,128)(2,1)S(1)}, u32[]{:S(2)}, u32[]{:S(2)}) collective-permute-start(bf16[2,16,8,2,16,128]{5,4,3,2,1,0:T(8,128)(2,1)S(1)} %bitcast.6), channel_id=1, source_target_pairs={{0,16},{16,0},{32,48},{48,32},{64,80},{80,64},{96,112},{112,96},{1... | collective-permute-start | bytes 6291464 | tf_op jit(solution)/shard_map/ppermute | solution.py:226
  126.0 25.7 %collective-permute-start.7 = (bf16[2,4,128,128]{3,2,1,0:T(8,128)(2,1)S(1)}, bf16[2,4,128,128]{3,2,1,0:T(8,128)(2,1)S(1)}, u32[]{:S(2)}, u32[]{:S(2)}) collective-permute-start(bf16[2,4,128,128]{3,2,1,0:T(8,128)(2,1)S(1)} %get-tuple-element.27), channel_id=1, source_target_pairs={{0,32},{16,48},{32,0},{48,16},{64,96},{80,112},{96,64},{112,80},{1... | collective-permute-start | bytes 786440 | tf_op jit(solution)/shard_map/ppermute | solution.py:226
  133.7 28.7 %collective-permute-start.8 = (bf16[2,4,128,128]{3,2,1,0:T(8,128)(2,1)S(1)}, bf16[2,4,128,128]{3,2,1,0:T(8,128)(2,1)S(1)}, u32[]{:S(2)}, u32[]{:S(2)}) collective-permute-start(bf16[2,4,128,128]{3,2,1,0:T(8,128)(2,1)S(1)} %get-tuple-element.28), channel_id=1, source_target_pairs={{0,96},{16,112},{32,64},{48,80},{64,32},{80,48},{96,0},{112,16},{1... | collective-permute-start | bytes 786440 | tf_op jit(solution)/shard_map/ppermute | solution.py:226

commit v3 on v2

--- a/solution.py
+++ b/solution.py
@@ -167,31 +167,28 @@
     )(position, both, both, both_swapped, both_swapped)
 
 
-def between_kernel(position, *refs):
-    far, side, (to_far, to_side) = refs[:NF], refs[NF : NF + NZ], refs[NF + NZ :]
-    for out, a, b in ((to_far, far, side), (to_side, side, far)):
-        found = cross(left_side(a), right_side(b))
-        for e in range(2):
-            out[e, 0] = found[:, e * CB : (e + 1) * CB]
+def between_kernel(position, both, *refs):
+    sides, (to_far, to_side) = refs[:NZ], refs[NZ:]
+    for k in range(HB):
+        far = [both.at[1 - position[2], g ^ position[1], k] for g in range(NF)]
+        side = [ref.at[:, k] for ref in sides]
+        for out, a, b in ((to_far, far, side), (to_side, side, far)):
+            found = cross(left_side(a), right_side(b))
+            for e in range(2):
+                out[e, k] = found[:, e * CB : (e + 1) * CB]
 
 
 def between(position, both, side):
-    far = [
-        pl.BlockSpec((1, 1, 1, 2, WD, CB), lambda k, position, g=g: (1 - position[2], g ^ position[1], k, 0, 0, 0))
-        for g in range(NF)
-    ]
-    piece = pl.BlockSpec((NX, 1, 2, WD, CB), lambda k, position: (0, k, 0, 0, 0))
-    out = pl.BlockSpec((2, 1, CB, CB), lambda k, position: (0, k, 0, 0))
+    vmem = pl.BlockSpec(memory_space=pltpu.VMEM)
     shape = jax.ShapeDtypeStruct((2, HB, CB, CB), jnp.bfloat16)
     return pl.pallas_call(
         between_kernel,
         out_shape=(shape, shape),
-        grid_spec=pltpu.PrefetchScalarGridSpec(
-            num_scalar_prefetch=1, grid=(HB,), in_specs=far + [piece] * NZ, out_specs=(out, out)
-        ),
+        in_specs=[pl.BlockSpec(memory_space=pltpu.SMEM)] + [vmem] * (1 + NZ),
+        out_specs=(vmem, vmem),
         compiler_params=pltpu.CompilerParams(vmem_limit_bytes=40 * MIB),
         name="between",
-    )(position, *[both] * NF, *side)
+    )(position, both, *side)
 
 
 def place_kernel(position, first, second, base, out):

time: 164 us -> 163 us (level)
  no operation moved by 1% of the time
where the time goes in v3:
time: 163 us
  waiting for transfers between devices  84.9 us (52%)
  starting transfers between devices  61.8 us (38%)
  Pallas kernels  15.7 us (10%)
    ppermute x7, waiting for transfers between devices, send(): return lax.ppermute(block, ('chan', 'freq'), moves)  52.7 us
    ppermute x7, starting transfers between devices, send(): return lax.ppermute(block, ('chan', 'freq'), moves)  32.3 us
    ppermute x3, waiting for transfers between devices, partner(): return lax.ppermute(block, 'chan', [(i, i ^ mask) for i in range(count)])  19.2 us
    all_to_all x1, starting transfers between devices, per_device(): lax.all_to_all(white.reshape((2 * NF,) + white.shape[2:]), ('chan', 'freq...  15.6 us
    ppermute x3, starting transfers between devices, partner(): return lax.ppermute(block, 'chan', [(i, i ^ mask) for i in range(count)])  13.9 us
    all_to_all x1, waiting for transfers between devices, per_device(): lax.all_to_all(white.reshape((2 * NF,) + white.shape[2:]), ('chan', 'freq...  13 us
    pallas_call x1, Pallas kernels, front(): pl.pallas_call(front_kernel, out_shape=(pltpu.HBM((2, NF, KL, 2, WD, CB),...  8.11 us
    pallas_call x1, Pallas kernels, rounds(): pl.pallas_call(rounds_kernel, out_shape=jax.ShapeDtypeStruct((ROUNDS, 2,...  5.2 us
  transfers between devices with their start and end apart: 11, of which 7 were waited for; matrix products, arithmetic and copies ran while one was open for 0% of the time, Pallas kernels for 4%

profile of v3, /device:TPU:6, one launch (start us, length us, event | category | flops | bytes accessed | tf_op | source)
XLA Modules:
  0.0 162.9 jit_solution(16720583098944792619)
XLA Ops:
  0.0 0.1 pad_add_fusion.position
  0.1 8.1 %white.1 = (bf16[2,16,8,2,16,128]{5,4,3,2,1,0:T(8,128)(2,1)}, bf16[4,4,2,16,128]{4,3,2,1,0:T(8,128)(2,1)S(1)}, bf16[4,4,2,16,128]{4,3,2,1,0:T(8,128)(2,1)S(1)}, ...) custom-call(s32[3]{0:T(128)S(1)} %pad_add_fusion.position, s32[16]{0:T(128)} %starts_in.1, ...), custom_call_target="tpu_custom_call" | custom-call | tf_op jit(solution)/shard_map/white/pallas_call | solution.py:102
  8.2 15.6 %all-to-all-start = ((bf16[32,8,2,16,128]{4,3,2,1,0:T(8,128)(2,1)}), bf16[32,8,2,16,128]{4,3,2,1,0:T(8,128)(2,1)S(1)}, u32[]{:S(2)}, u32[]{:S(2)}) async-start(bf16[32,8,2,16,128]{4,3,2,1,0:T(8,128)(2,1)} %bitcast.10), calls=%async_computation | async-start | bytes 4194304 | tf_op jit(solution)/shard_map/all_to_all | solution.py:250
  23.8 2.8 %collective-permute-start = (bf16[4,4,2,16,128]{4,3,2,1,0:T(8,128)(2,1)S(1)}, bf16[4,4,2,16,128]{4,3,2,1,0:T(8,128)(2,1)S(1)}, u32[]{:S(2)}, u32[]{:S(2)}) collective-permute-start(bf16[4,4,2,16,128]{4,3,2,1,0:T(8,128)(2,1)S(1)} %get-tuple-element.19), channel_id=1, source_target_pairs={{0,1},{1,0},{2,3},{3,2},{4,5},{5,4},{6,7},{7,6},{8,9},{9,8},{10,11... | collective-permute-start | bytes 393224 | tf_op jit(solution)/shard_map/ppermute | solution.py:231
  26.6 2.7 %collective-permute-start.1 = (bf16[4,4,2,16,128]{4,3,2,1,0:T(8,128)(2,1)S(1)}, bf16[4,4,2,16,128]{4,3,2,1,0:T(8,128)(2,1)S(1)}, u32[]{:S(2)}, u32[]{:S(2)}) collective-permute-start(bf16[4,4,2,16,128]{4,3,2,1,0:T(8,128)(2,1)S(1)} %get-tuple-element.20), channel_id=1, source_target_pairs={{0,2},{1,3},{2,0},{3,1},{4,6},{5,7},{6,4},{7,5},{8,10},{9,11},{10,... | collective-permute-start | bytes 393224 | tf_op jit(solution)/shard_map/ppermute | solution.py:231
  29.3 4.9 %collective-permute-start.2 = (bf16[4,4,2,16,128]{4,3,2,1,0:T(8,128)(2,1)S(1)}, bf16[4,4,2,16,128]{4,3,2,1,0:T(8,128)(2,1)S(1)}, u32[]{:S(2)}, u32[]{:S(2)}) collective-permute-start(bf16[4,4,2,16,128]{4,3,2,1,0:T(8,128)(2,1)S(1)} %get-tuple-element.21), channel_id=1, source_target_pairs={{0,3},{1,2},{2,1},{3,0},{4,7},{5,6},{6,5},{7,4},{8,11},{9,10},{10,... | collective-permute-start | bytes 393224 | tf_op jit(solution)/shard_map/ppermute | solution.py:231
  34.3 1.9 %collective-permute-done = bf16[4,4,2,16,128]{4,3,2,1,0:T(8,128)(2,1)S(1)} collective-permute-done((bf16[4,4,2,16,128]{4,3,2,1,0:T(8,128)(2,1)S(1)}, bf16[4,4,2,16,128]{4,3,2,1,0:T(8,128)(2,1)S(1)}, u32[]{:S(2)}, u32[]{:S(2)}) %collective-permute-start) | collective-permute-done | bytes 131104 | tf_op jit(solution)/shard_map/ppermute | solution.py:231
  36.2 4.3 %collective-permute-done.1 = bf16[4,4,2,16,128]{4,3,2,1,0:T(8,128)(2,1)S(1)} collective-permute-done((bf16[4,4,2,16,128]{4,3,2,1,0:T(8,128)(2,1)S(1)}, bf16[4,4,2,16,128]{4,3,2,1,0:T(8,128)(2,1)S(1)}, u32[]{:S(2)}, u32[]{:S(2)}) %collective-permute-start.1) | collective-permute-done | bytes 131104 | tf_op jit(solution)/shard_map/ppermute | solution.py:231
  40.5 2.6 %collective-permute-done.2 = bf16[4,4,2,16,128]{4,3,2,1,0:T(8,128)(2,1)S(1)} collective-permute-done((bf16[4,4,2,16,128]{4,3,2,1,0:T(8,128)(2,1)S(1)}, bf16[4,4,2,16,128]{4,3,2,1,0:T(8,128)(2,1)S(1)}, u32[]{:S(2)}, u32[]{:S(2)}) %collective-permute-start.2) | collective-permute-done | bytes 131104 | tf_op jit(solution)/shard_map/ppermute | solution.py:231
  43.1 5.7 %collective-permute-start.3 = (bf16[4,4,2,16,128]{4,3,2,1,0:T(8,128)(2,1)S(1)}, bf16[4,4,2,16,128]{4,3,2,1,0:T(8,128)(2,1)S(1)}, u32[]{:S(2)}, u32[]{:S(2)}) collective-permute-start(bf16[4,4,2,16,128]{4,3,2,1,0:T(8,128)(2,1)S(1)} %pad_maximum_fusion), channel_id=1, source_target_pairs={{0,96},{1,97},{2,98},{3,99},{4,100},{5,101},{6,102},{7,103},{8,104... | collective-permute-start | bytes 393224 | tf_op jit(solution)/shard_map/ppermute | solution.py:231
  48.9 3.5 %collective-permute-start.4 = (bf16[4,4,2,16,128]{4,3,2,1,0:T(8,128)(2,1)S(1)}, bf16[4,4,2,16,128]{4,3,2,1,0:T(8,128)(2,1)S(1)}, u32[]{:S(2)}, u32[]{:S(2)}) collective-permute-start(bf16[4,4,2,16,128]{4,3,2,1,0:T(8,128)(2,1)S(1)} %pad_maximum_fusion.1), channel_id=1, source_target_pairs={{0,100},{1,101},{2,102},{3,103},{4,96},{5,97},{6,98},{7,99},{8,108... | collective-permute-start | bytes 393224 | tf_op jit(solution)/shard_map/ppermute | solution.py:231
  52.4 10.8 %collective-permute-start.5 = (bf16[4,4,2,16,128]{4,3,2,1,0:T(8,128)(2,1)S(1)}, bf16[4,4,2,16,128]{4,3,2,1,0:T(8,128)(2,1)S(1)}, u32[]{:S(2)}, u32[]{:S(2)}) collective-permute-start(bf16[4,4,2,16,128]{4,3,2,1,0:T(8,128)(2,1)S(1)} %pad_maximum_fusion.2), channel_id=1, source_target_pairs={{0,104},{1,105},{2,106},{3,107},{4,108},{5,109},{6,110},{7,111},{8... | collective-permute-start | bytes 393224 | tf_op jit(solution)/shard_map/ppermute | solution.py:231
  63.2 1.9 %collective-permute-start.6 = (bf16[4,4,2,16,128]{4,3,2,1,0:T(8,128)(2,1)S(1)}, bf16[4,4,2,16,128]{4,3,2,1,0:T(8,128)(2,1)S(1)}, u32[]{:S(2)}, u32[]{:S(2)}) collective-permute-start(bf16[4,4,2,16,128]{4,3,2,1,0:T(8,128)(2,1)S(1)} %pad_maximum_fusion.3), channel_id=1, source_target_pairs={{0,108},{1,109},{2,110},{3,111},{4,104},{5,105},{6,106},{7,107},{8... | collective-permute-start | bytes 393224 | tf_op jit(solution)/shard_map/ppermute | solution.py:231
  65.1 43.9 %collective-permute-done.3.refs_0_ = bf16[4,4,2,16,128]{4,3,2,1,0:T(8,128)(2,1)S(1)} collective-permute-done((bf16[4,4,2,16,128]{4,3,2,1,0:T(8,128)(2,1)S(1)}, bf16[4,4,2,16,128]{4,3,2,1,0:T(8,128)(2,1)S(1)}, u32[]{:S(2)}, u32[]{:S(2)}) %collective-permute-start.3) | collective-permute-done | bytes 131104 | tf_op jit(solution)/shard_map/ppermute | solution.py:231
  109.0 0.0 collective-permute-done.4.refs_1_
  109.0 0.0 collective-permute-done.5.refs_2_
  109.0 0.0 collective-permute-done.6.refs_3_
  109.0 13.0 %all-to-all-done = bf16[32,8,2,16,128]{4,3,2,1,0:T(8,128)(2,1)S(1)} async-done(((bf16[32,8,2,16,128]{4,3,2,1,0:T(8,128)(2,1)}), bf16[32,8,2,16,128]{4,3,2,1,0:T(8,128)(2,1)S(1)}, u32[]{:S(2)}, u32[]{:S(2)}) %all-to-all-start) | async-done | bytes 2097184 | tf_op jit(solution)/shard_map/all_to_all | solution.py:250
  122.0 1.9 %collective-permute-start.9 = (bf16[2,16,8,2,16,128]{5,4,3,2,1,0:T(8,128)(2,1)S(1)}, bf16[2,16,8,2,16,128]{5,4,3,2,1,0:T(8,128)(2,1)S(1)}, u32[]{:S(2)}, u32[]{:S(2)}) collective-permute-start(bf16[2,16,8,2,16,128]{5,4,3,2,1,0:T(8,128)(2,1)S(1)} %bitcast.6), channel_id=1, source_target_pairs={{0,16},{16,0},{32,48},{48,32},{64,80},{80,64},{96,112},{112,96},{1... | collective-permute-start | bytes 6291464 | tf_op jit(solution)/shard_map/ppermute | solution.py:223
  124.0 1.0 between.1
  125.0 7.7 %collective-permute-start.7 = (bf16[2,4,128,128]{3,2,1,0:T(8,128)(2,1)S(1)}, bf16[2,4,128,128]{3,2,1,0:T(8,128)(2,1)S(1)}, u32[]{:S(2)}, u32[]{:S(2)}) collective-permute-start(bf16[2,4,128,128]{3,2,1,0:T(8,128)(2,1)S(1)} %get-tuple-element.27), channel_id=1, source_target_pairs={{0,32},{16,48},{32,0},{48,16},{64,96},{80,112},{96,64},{112,80},{1... | collective-permute-start | bytes 786440 | tf_op jit(solution)/shard_map/ppermute | solution.py:223
  132.8 4.3 %collective-permute-start.8 = (bf16[2,4,128,128]{3,2,1,0:T(8,128)(2,1)S(1)}, bf16[2,4,128,128]{3,2,1,0:T(8,128)(2,1)S(1)}, u32[]{:S(2)}, u32[]{:S(2)}) collective-permute-start(bf16[2,4,128,128]{3,2,1,0:T(8,128)(2,1)S(1)} %get-tuple-element.28), channel_id=1, source_target_pairs={{0,96},{16,112},{32,64},{48,80},{64,32},{80,48},{96,0},{112,16},{1... | collective-permute-start | bytes 786440 | tf_op jit(solution)/shard_map/ppermute | solution.py:223
  137.0 0.0 collective-permute-done.9.own_swapped.far_swapped
  137.0 5.2 %rounds.1.base = bf16[4,2,8,128,128]{4,3,2,1,0:T(8,128)(2,1)} custom-call(s32[3]{0:T(128)S(1)} %pad_add_fusion.position, bf16[2,16,8,2,16,128]{5,4,3,2,1,0:T(8,128)(2,1)S(1)} %bitcast.8, bf16[2,16,8,2,16,128]{5,4,3,2,1,0:T(8,128)(2,1)S(1)} %bitcast.9, bf16[2,16,8,2,16,128]{5,4,3,2,1,0:T(8,128)(2,1)S(1)} %collective-permute-done.9.own_swapped.far_swapped, ...), custom_call_target="tpu_custom_call" | custom-call | tf_op jit(solution)/shard_map/rounds/pallas_call | solution.py:156
  142.2 8.5 %collective-permute-done.7.first = bf16[2,4,128,128]{3,2,1,0:T(8,128)(2,1)S(1)} collective-permute-done((bf16[2,4,128,128]{3,2,1,0:T(8,128)(2,1)S(1)}, bf16[2,4,128,128]{3,2,1,0:T(8,128)(2,1)S(1)}, u32[]{:S(2)}, u32[]{:S(2)}) %collective-permute-start.7) | collective-permute-done | bytes 262176 | tf_op jit(solution)/shard_map/ppermute | solution.py:223
  150.8 10.7 %collective-permute-done.8.second = bf16[2,4,128,128]{3,2,1,0:T(8,128)(2,1)S(1)} collective-permute-done((bf16[2,4,128,128]{3,2,1,0:T(8,128)(2,1)S(1)}, bf16[2,4,128,128]{3,2,1,0:T(8,128)(2,1)S(1)}, u32[]{:S(2)}, u32[]{:S(2)}) %collective-permute-start.8) | collective-permute-done | bytes 262176 | tf_op jit(solution)/shard_map/ppermute | solution.py:223
  161.5 1.4 place.1
  (8 shorter events, 0.1 us)
Async XLA Ops:
  8.2 113.8 %all-to-all-start = ((bf16[32,8,2,16,128]{4,3,2,1,0:T(8,128)(2,1)}), bf16[32,8,2,16,128]{4,3,2,1,0:T(8,128)(2,1)S(1)}, u32[]{:S(2)}, u32[]{:S(2)}) async-start(bf16[32,8,2,16,128]{4,3,2,1,0:T(8,128)(2,1)} %bitcast.10), calls=%async_computation | async-start | bytes 4194304 | tf_op jit(solution)/shard_map/all_to_all | solution.py:250
  23.8 12.4 %collective-permute-start = (bf16[4,4,2,16,128]{4,3,2,1,0:T(8,128)(2,1)S(1)}, bf16[4,4,2,16,128]{4,3,2,1,0:T(8,128)(2,1)S(1)}, u32[]{:S(2)}, u32[]{:S(2)}) collective-permute-start(bf16[4,4,2,16,128]{4,3,2,1,0:T(8,128)(2,1)S(1)} %get-tuple-element.19), channel_id=1, source_target_pairs={{0,1},{1,0},{2,3},{3,2},{4,5},{5,4},{6,7},{7,6},{8,9},{9,8},{10,11... | collective-permute-start | bytes 393224 | tf_op jit(solution)/shard_map/ppermute | solution.py:231
  26.6 13.9 %collective-permute-start.1 = (bf16[4,4,2,16,128]{4,3,2,1,0:T(8,128)(2,1)S(1)}, bf16[4,4,2,16,128]{4,3,2,1,0:T(8,128)(2,1)S(1)}, u32[]{:S(2)}, u32[]{:S(2)}) collective-permute-start(bf16[4,4,2,16,128]{4,3,2,1,0:T(8,128)(2,1)S(1)} %get-tuple-element.20), channel_id=1, source_target_pairs={{0,2},{1,3},{2,0},{3,1},{4,6},{5,7},{6,4},{7,5},{8,10},{9,11},{10,... | collective-permute-start | bytes 393224 | tf_op jit(solution)/shard_map/ppermute | solution.py:231
  29.3 13.7 %collective-permute-start.2 = (bf16[4,4,2,16,128]{4,3,2,1,0:T(8,128)(2,1)S(1)}, bf16[4,4,2,16,128]{4,3,2,1,0:T(8,128)(2,1)S(1)}, u32[]{:S(2)}, u32[]{:S(2)}) collective-permute-start(bf16[4,4,2,16,128]{4,3,2,1,0:T(8,128)(2,1)S(1)} %get-tuple-element.21), channel_id=1, source_target_pairs={{0,3},{1,2},{2,1},{3,0},{4,7},{5,6},{6,5},{7,4},{8,11},{9,10},{10,... | collective-permute-start | bytes 393224 | tf_op jit(solution)/shard_map/ppermute | solution.py:231
  43.1 65.9 %collective-permute-start.3 = (bf16[4,4,2,16,128]{4,3,2,1,0:T(8,128)(2,1)S(1)}, bf16[4,4,2,16,128]{4,3,2,1,0:T(8,128)(2,1)S(1)}, u32[]{:S(2)}, u32[]{:S(2)}) collective-permute-start(bf16[4,4,2,16,128]{4,3,2,1,0:T(8,128)(2,1)S(1)} %pad_maximum_fusion), channel_id=1, source_target_pairs={{0,96},{1,97},{2,98},{3,99},{4,100},{5,101},{6,102},{7,103},{8,104... | collective-permute-start | bytes 393224 | tf_op jit(solution)/shard_map/ppermute | solution.py:231
  48.9 60.1 %collective-permute-start.4 = (bf16[4,4,2,16,128]{4,3,2,1,0:T(8,128)(2,1)S(1)}, bf16[4,4,2,16,128]{4,3,2,1,0:T(8,128)(2,1)S(1)}, u32[]{:S(2)}, u32[]{:S(2)}) collective-permute-start(bf16[4,4,2,16,128]{4,3,2,1,0:T(8,128)(2,1)S(1)} %pad_maximum_fusion.1), channel_id=1, source_target_pairs={{0,100},{1,101},{2,102},{3,103},{4,96},{5,97},{6,98},{7,99},{8,108... | collective-permute-start | bytes 393224 | tf_op jit(solution)/shard_map/ppermute | solution.py:231
  52.4 56.6 %collective-permute-start.5 = (bf16[4,4,2,16,128]{4,3,2,1,0:T(8,128)(2,1)S(1)}, bf16[4,4,2,16,128]{4,3,2,1,0:T(8,128)(2,1)S(1)}, u32[]{:S(2)}, u32[]{:S(2)}) collective-permute-start(bf16[4,4,2,16,128]{4,3,2,1,0:T(8,128)(2,1)S(1)} %pad_maximum_fusion.2), channel_id=1, source_target_pairs={{0,104},{1,105},{2,106},{3,107},{4,108},{5,109},{6,110},{7,111},{8... | collective-permute-start | bytes 393224 | tf_op jit(solution)/shard_map/ppermute | solution.py:231
  63.2 45.8 %collective-permute-start.6 = (bf16[4,4,2,16,128]{4,3,2,1,0:T(8,128)(2,1)S(1)}, bf16[4,4,2,16,128]{4,3,2,1,0:T(8,128)(2,1)S(1)}, u32[]{:S(2)}, u32[]{:S(2)}) collective-permute-start(bf16[4,4,2,16,128]{4,3,2,1,0:T(8,128)(2,1)S(1)} %pad_maximum_fusion.3), channel_id=1, source_target_pairs={{0,108},{1,109},{2,110},{3,111},{4,104},{5,105},{6,106},{7,107},{8... | collective-permute-start | bytes 393224 | tf_op jit(solution)/shard_map/ppermute | solution.py:231
  122.0 15.0 %collective-permute-start.9 = (bf16[2,16,8,2,16,128]{5,4,3,2,1,0:T(8,128)(2,1)S(1)}, bf16[2,16,8,2,16,128]{5,4,3,2,1,0:T(8,128)(2,1)S(1)}, u32[]{:S(2)}, u32[]{:S(2)}) collective-permute-start(bf16[2,16,8,2,16,128]{5,4,3,2,1,0:T(8,128)(2,1)S(1)} %bitcast.6), channel_id=1, source_target_pairs={{0,16},{16,0},{32,48},{48,32},{64,80},{80,64},{96,112},{112,96},{1... | collective-permute-start | bytes 6291464 | tf_op jit(solution)/shard_map/ppermute | solution.py:223
  125.0 25.8 %collective-permute-start.7 = (bf16[2,4,128,128]{3,2,1,0:T(8,128)(2,1)S(1)}, bf16[2,4,128,128]{3,2,1,0:T(8,128)(2,1)S(1)}, u32[]{:S(2)}, u32[]{:S(2)}) collective-permute-start(bf16[2,4,128,128]{3,2,1,0:T(8,128)(2,1)S(1)} %get-tuple-element.27), channel_id=1, source_target_pairs={{0,32},{16,48},{32,0},{48,16},{64,96},{80,112},{96,64},{112,80},{1... | collective-permute-start | bytes 786440 | tf_op jit(solution)/shard_map/ppermute | solution.py:223
  132.8 28.7 %collective-permute-start.8 = (bf16[2,4,128,128]{3,2,1,0:T(8,128)(2,1)S(1)}, bf16[2,4,128,128]{3,2,1,0:T(8,128)(2,1)S(1)}, u32[]{:S(2)}, u32[]{:S(2)}) collective-permute-start(bf16[2,4,128,128]{3,2,1,0:T(8,128)(2,1)S(1)} %get-tuple-element.28), channel_id=1, source_target_pairs={{0,96},{16,112},{32,64},{48,80},{64,32},{80,48},{96,0},{112,16},{1... | collective-permute-start | bytes 786440 | tf_op jit(solution)/shard_map/ppermute | solution.py:223

commit v4 on v3

--- a/solution.py
+++ b/solution.py
@@ -54,7 +54,8 @@
             table[part * K : (part + 1) * K, block * K : (block + 1) * K] = cosine(phase).astype(jnp.bfloat16)
     copies[1].wait()
     copies[2].wait()
-    wide[...] = held[...].astype(jnp.float32)
+    wide[:SEG, :] = held[...].astype(jnp.float32)
+    wide[SEG:, :] = jnp.zeros((2 * WD, CB), jnp.float32)
     for pair in range(WD // 2):
         slot = tapered.at[pair % 2]
         for side in range(2):
@@ -73,7 +74,7 @@
         part = spectra[pl.ds(pl.multiple_of(f * rows, rows), rows), :].reshape(2 * KL, WD, CB)
         return power + jnp.sum(part * part, axis=0)
 
-    power = lax.fori_loop(0, NF, add, jnp.zeros((WD, CB), jnp.float32))
+    power = lax.fori_loop(0, NF, add, jnp.zeros((WD, CB), jnp.float32), unroll=4)
     gain = lax.rsqrt(power * (1.0 / (2 * K)) + 1e-6)[None]
 
     def whiten(f, carry):
@@ -85,7 +86,7 @@
             pltpu.make_async_copy(ready.at[f], white.at[number, f], out_sems.at[number]).start()
         return carry
 
-    lax.fori_loop(0, NF, whiten, 0)
+    lax.fori_loop(0, NF, whiten, 0, unroll=4)
     for e, out in enumerate(crossed):
         for d in range(NZ):
             out[d] = ready[(d * NX + e) ^ position[1], HB:]
@@ -109,11 +110,11 @@
             pltpu.SMEM((WD,), jnp.int32),
             pltpu.VMEM((1, K), jnp.int32),
             pltpu.VMEM((SEG, CB), jnp.bfloat16),
-            pltpu.VMEM((SEG, CB), jnp.float32),
+            pltpu.VMEM((SEG + 2 * WD, CB), jnp.float32),
             pltpu.VMEM((L, CB), jnp.float32),
             pltpu.VMEM((2 * K, L), jnp.bfloat16),
             pltpu.VMEM((2, L, 2 * CB), jnp.bfloat16),
-            pltpu.VMEM((2 * K * WD, CB), jnp.float32),
+            pltpu.VMEM((2 * K * WD + 2 * WD, CB), jnp.float32),
             pltpu.VMEM((NF, KL, 2, WD, CB), jnp.bfloat16),
             pltpu.SemaphoreType.DMA((3,)),
             pltpu.SemaphoreType.DMA((2,)),
@@ -172,10 +173,12 @@
     for k in range(HB):
         far = [both.at[1 - position[2], g ^ position[1], k] for g in range(NF)]
         side = [ref.at[:, k] for ref in sides]
-        for out, a, b in ((to_far, far, side), (to_side, side, far)):
-            found = cross(left_side(a), right_side(b))
-            for e in range(2):
-                out[e, k] = found[:, e * CB : (e + 1) * CB]
+        left, right = (jnp.concatenate([part_of(refs, 0), part_of(refs, 1)], axis=1) for refs in (far, side))
+        found = lax.dot_general(left, right, (((0,), (0,)), ((), ())), preferred_element_type=jnp.float32)
+        real = (found[:CB, :CB] + found[CB:, CB:]) * SCALE
+        imag = (found[CB:, :CB] - found[:CB, CB:]) * SCALE
+        to_far[0, k], to_far[1, k] = real.astype(jnp.bfloat16), imag.astype(jnp.bfloat16)
+        to_side[0, k], to_side[1, k] = real.T.astype(jnp.bfloat16), (-imag).T.astype(jnp.bfloat16)
 
 
 def between(position, both, side):

time: 163 us -> 163 us (level)
  no operation moved by 1% of the time
where the time goes in v4:
time: 163 us
  waiting for transfers between devices  84.9 us (52%)
  starting transfers between devices  61.9 us (38%)
  Pallas kernels  15.4 us (9%)
    ppermute x7, waiting for transfers between devices, send(): return lax.ppermute(block, ('chan', 'freq'), moves)  52.7 us
    ppermute x7, starting transfers between devices, send(): return lax.ppermute(block, ('chan', 'freq'), moves)  32.3 us
    ppermute x3, waiting for transfers between devices, partner(): return lax.ppermute(block, 'chan', [(i, i ^ mask) for i in range(count)])  19.2 us
    all_to_all x1, starting transfers between devices, per_device(): lax.all_to_all(white.reshape((2 * NF,) + white.shape[2:]), ('chan', 'freq...  15.6 us
    ppermute x3, starting transfers between devices, partner(): return lax.ppermute(block, 'chan', [(i, i ^ mask) for i in range(count)])  13.9 us
    all_to_all x1, waiting for transfers between devices, per_device(): lax.all_to_all(white.reshape((2 * NF,) + white.shape[2:]), ('chan', 'freq...  13 us
    pallas_call x1, Pallas kernels, front(): pl.pallas_call(front_kernel, out_shape=(pltpu.HBM((2, NF, KL, 2, WD, CB),...  7.89 us
    pallas_call x1, Pallas kernels, rounds(): pl.pallas_call(rounds_kernel, out_shape=jax.ShapeDtypeStruct((ROUNDS, 2,...  5.19 us
  transfers between devices with their start and end apart: 11, of which 7 were waited for; matrix products, arithmetic and copies ran while one was open for 0% of the time, Pallas kernels for 4%

profile of v4, /device:TPU:6, one launch (start us, length us, event | category | flops | bytes accessed | tf_op | source)
XLA Modules:
  0.0 162.5 jit_solution(1987387940783454131)
XLA Ops:
  0.0 0.1 pad_add_fusion.position
  0.1 7.9 %white.1 = (bf16[2,16,8,2,16,128]{5,4,3,2,1,0:T(8,128)(2,1)}, bf16[4,4,2,16,128]{4,3,2,1,0:T(8,128)(2,1)S(1)}, bf16[4,4,2,16,128]{4,3,2,1,0:T(8,128)(2,1)S(1)}, ...) custom-call(s32[3]{0:T(128)S(1)} %pad_add_fusion.position, s32[16]{0:T(128)} %starts_in.1, ...), custom_call_target="tpu_custom_call" | custom-call | tf_op jit(solution)/shard_map/white/pallas_call | solution.py:103
  8.0 15.6 %all-to-all-start = ((bf16[32,8,2,16,128]{4,3,2,1,0:T(8,128)(2,1)}), bf16[32,8,2,16,128]{4,3,2,1,0:T(8,128)(2,1)S(1)}, u32[]{:S(2)}, u32[]{:S(2)}) async-start(bf16[32,8,2,16,128]{4,3,2,1,0:T(8,128)(2,1)} %bitcast.10), calls=%async_computation | async-start | bytes 4194304 | tf_op jit(solution)/shard_map/all_to_all | solution.py:253
  23.6 2.8 %collective-permute-start = (bf16[4,4,2,16,128]{4,3,2,1,0:T(8,128)(2,1)S(1)}, bf16[4,4,2,16,128]{4,3,2,1,0:T(8,128)(2,1)S(1)}, u32[]{:S(2)}, u32[]{:S(2)}) collective-permute-start(bf16[4,4,2,16,128]{4,3,2,1,0:T(8,128)(2,1)S(1)} %get-tuple-element.19), channel_id=1, source_target_pairs={{0,1},{1,0},{2,3},{3,2},{4,5},{5,4},{6,7},{7,6},{8,9},{9,8},{10,11... | collective-permute-start | bytes 393224 | tf_op jit(solution)/shard_map/ppermute | solution.py:234
  26.4 2.7 %collective-permute-start.1 = (bf16[4,4,2,16,128]{4,3,2,1,0:T(8,128)(2,1)S(1)}, bf16[4,4,2,16,128]{4,3,2,1,0:T(8,128)(2,1)S(1)}, u32[]{:S(2)}, u32[]{:S(2)}) collective-permute-start(bf16[4,4,2,16,128]{4,3,2,1,0:T(8,128)(2,1)S(1)} %get-tuple-element.20), channel_id=1, source_target_pairs={{0,2},{1,3},{2,0},{3,1},{4,6},{5,7},{6,4},{7,5},{8,10},{9,11},{10,... | collective-permute-start | bytes 393224 | tf_op jit(solution)/shard_map/ppermute | solution.py:234
  29.1 4.9 %collective-permute-start.2 = (bf16[4,4,2,16,128]{4,3,2,1,0:T(8,128)(2,1)S(1)}, bf16[4,4,2,16,128]{4,3,2,1,0:T(8,128)(2,1)S(1)}, u32[]{:S(2)}, u32[]{:S(2)}) collective-permute-start(bf16[4,4,2,16,128]{4,3,2,1,0:T(8,128)(2,1)S(1)} %get-tuple-element.21), channel_id=1, source_target_pairs={{0,3},{1,2},{2,1},{3,0},{4,7},{5,6},{6,5},{7,4},{8,11},{9,10},{10,... | collective-permute-start | bytes 393224 | tf_op jit(solution)/shard_map/ppermute | solution.py:234
  34.0 1.9 %collective-permute-done = bf16[4,4,2,16,128]{4,3,2,1,0:T(8,128)(2,1)S(1)} collective-permute-done((bf16[4,4,2,16,128]{4,3,2,1,0:T(8,128)(2,1)S(1)}, bf16[4,4,2,16,128]{4,3,2,1,0:T(8,128)(2,1)S(1)}, u32[]{:S(2)}, u32[]{:S(2)}) %collective-permute-start) | collective-permute-done | bytes 131104 | tf_op jit(solution)/shard_map/ppermute | solution.py:234
  36.0 4.2 %collective-permute-done.1 = bf16[4,4,2,16,128]{4,3,2,1,0:T(8,128)(2,1)S(1)} collective-permute-done((bf16[4,4,2,16,128]{4,3,2,1,0:T(8,128)(2,1)S(1)}, bf16[4,4,2,16,128]{4,3,2,1,0:T(8,128)(2,1)S(1)}, u32[]{:S(2)}, u32[]{:S(2)}) %collective-permute-start.1) | collective-permute-done | bytes 131104 | tf_op jit(solution)/shard_map/ppermute | solution.py:234
  40.2 2.6 %collective-permute-done.2 = bf16[4,4,2,16,128]{4,3,2,1,0:T(8,128)(2,1)S(1)} collective-permute-done((bf16[4,4,2,16,128]{4,3,2,1,0:T(8,128)(2,1)S(1)}, bf16[4,4,2,16,128]{4,3,2,1,0:T(8,128)(2,1)S(1)}, u32[]{:S(2)}, u32[]{:S(2)}) %collective-permute-start.2) | collective-permute-done | bytes 131104 | tf_op jit(solution)/shard_map/ppermute | solution.py:234
  42.9 5.7 %collective-permute-start.3 = (bf16[4,4,2,16,128]{4,3,2,1,0:T(8,128)(2,1)S(1)}, bf16[4,4,2,16,128]{4,3,2,1,0:T(8,128)(2,1)S(1)}, u32[]{:S(2)}, u32[]{:S(2)}) collective-permute-start(bf16[4,4,2,16,128]{4,3,2,1,0:T(8,128)(2,1)S(1)} %pad_maximum_fusion), channel_id=1, source_target_pairs={{0,96},{1,97},{2,98},{3,99},{4,100},{5,101},{6,102},{7,103},{8,104... | collective-permute-start | bytes 393224 | tf_op jit(solution)/shard_map/ppermute | solution.py:234
  48.7 3.5 %collective-permute-start.4 = (bf16[4,4,2,16,128]{4,3,2,1,0:T(8,128)(2,1)S(1)}, bf16[4,4,2,16,128]{4,3,2,1,0:T(8,128)(2,1)S(1)}, u32[]{:S(2)}, u32[]{:S(2)}) collective-permute-start(bf16[4,4,2,16,128]{4,3,2,1,0:T(8,128)(2,1)S(1)} %pad_maximum_fusion.1), channel_id=1, source_target_pairs={{0,100},{1,101},{2,102},{3,103},{4,96},{5,97},{6,98},{7,99},{8,108... | collective-permute-start | bytes 393224 | tf_op jit(solution)/shard_map/ppermute | solution.py:234
  52.2 10.8 %collective-permute-start.5 = (bf16[4,4,2,16,128]{4,3,2,1,0:T(8,128)(2,1)S(1)}, bf16[4,4,2,16,128]{4,3,2,1,0:T(8,128)(2,1)S(1)}, u32[]{:S(2)}, u32[]{:S(2)}) collective-permute-start(bf16[4,4,2,16,128]{4,3,2,1,0:T(8,128)(2,1)S(1)} %pad_maximum_fusion.2), channel_id=1, source_target_pairs={{0,104},{1,105},{2,106},{3,107},{4,108},{5,109},{6,110},{7,111},{8... | collective-permute-start | bytes 393224 | tf_op jit(solution)/shard_map/ppermute | solution.py:234
  63.0 1.9 %collective-permute-start.6 = (bf16[4,4,2,16,128]{4,3,2,1,0:T(8,128)(2,1)S(1)}, bf16[4,4,2,16,128]{4,3,2,1,0:T(8,128)(2,1)S(1)}, u32[]{:S(2)}, u32[]{:S(2)}) collective-permute-start(bf16[4,4,2,16,128]{4,3,2,1,0:T(8,128)(2,1)S(1)} %pad_maximum_fusion.3), channel_id=1, source_target_pairs={{0,108},{1,109},{2,110},{3,111},{4,104},{5,105},{6,106},{7,107},{8... | collective-permute-start | bytes 393224 | tf_op jit(solution)/shard_map/ppermute | solution.py:234
  64.9 43.9 %collective-permute-done.3.refs_0_ = bf16[4,4,2,16,128]{4,3,2,1,0:T(8,128)(2,1)S(1)} collective-permute-done((bf16[4,4,2,16,128]{4,3,2,1,0:T(8,128)(2,1)S(1)}, bf16[4,4,2,16,128]{4,3,2,1,0:T(8,128)(2,1)S(1)}, u32[]{:S(2)}, u32[]{:S(2)}) %collective-permute-start.3) | collective-permute-done | bytes 131104 | tf_op jit(solution)/shard_map/ppermute | solution.py:234
  108.8 0.0 collective-permute-done.4.refs_1_
  108.8 0.0 collective-permute-done.5.refs_2_
  108.8 0.0 collective-permute-done.6.refs_3_
  108.8 13.0 %all-to-all-done = bf16[32,8,2,16,128]{4,3,2,1,0:T(8,128)(2,1)S(1)} async-done(((bf16[32,8,2,16,128]{4,3,2,1,0:T(8,128)(2,1)}), bf16[32,8,2,16,128]{4,3,2,1,0:T(8,128)(2,1)S(1)}, u32[]{:S(2)}, u32[]{:S(2)}) %all-to-all-start) | async-done | bytes 2097184 | tf_op jit(solution)/shard_map/all_to_all | solution.py:253
  121.8 1.9 %collective-permute-start.9 = (bf16[2,16,8,2,16,128]{5,4,3,2,1,0:T(8,128)(2,1)S(1)}, bf16[2,16,8,2,16,128]{5,4,3,2,1,0:T(8,128)(2,1)S(1)}, u32[]{:S(2)}, u32[]{:S(2)}) collective-permute-start(bf16[2,16,8,2,16,128]{5,4,3,2,1,0:T(8,128)(2,1)S(1)} %bitcast.6), channel_id=1, source_target_pairs={{0,16},{16,0},{32,48},{48,32},{64,80},{80,64},{96,112},{112,96},{1... | collective-permute-start | bytes 6291464 | tf_op jit(solution)/shard_map/ppermute | solution.py:226
  123.7 1.0 between.1
  124.7 7.7 %collective-permute-start.7 = (bf16[2,4,128,128]{3,2,1,0:T(8,128)(2,1)S(1)}, bf16[2,4,128,128]{3,2,1,0:T(8,128)(2,1)S(1)}, u32[]{:S(2)}, u32[]{:S(2)}) collective-permute-start(bf16[2,4,128,128]{3,2,1,0:T(8,128)(2,1)S(1)} %get-tuple-element.27), channel_id=1, source_target_pairs={{0,32},{16,48},{32,0},{48,16},{64,96},{80,112},{96,64},{112,80},{1... | collective-permute-start | bytes 786440 | tf_op jit(solution)/shard_map/ppermute | solution.py:226
  132.5 4.3 %collective-permute-start.8 = (bf16[2,4,128,128]{3,2,1,0:T(8,128)(2,1)S(1)}, bf16[2,4,128,128]{3,2,1,0:T(8,128)(2,1)S(1)}, u32[]{:S(2)}, u32[]{:S(2)}) collective-permute-start(bf16[2,4,128,128]{3,2,1,0:T(8,128)(2,1)S(1)} %get-tuple-element.28), channel_id=1, source_target_pairs={{0,96},{16,112},{32,64},{48,80},{64,32},{80,48},{96,0},{112,16},{1... | collective-permute-start | bytes 786440 | tf_op jit(solution)/shard_map/ppermute | solution.py:226
  136.7 0.0 collective-permute-done.9.own_swapped.far_swapped
  136.8 5.2 %rounds.1.base = bf16[4,2,8,128,128]{4,3,2,1,0:T(8,128)(2,1)} custom-call(s32[3]{0:T(128)S(1)} %pad_add_fusion.position, bf16[2,16,8,2,16,128]{5,4,3,2,1,0:T(8,128)(2,1)S(1)} %bitcast.8, bf16[2,16,8,2,16,128]{5,4,3,2,1,0:T(8,128)(2,1)S(1)} %bitcast.9, bf16[2,16,8,2,16,128]{5,4,3,2,1,0:T(8,128)(2,1)S(1)} %collective-permute-done.9.own_swapped.far_swapped, ...), custom_call_target="tpu_custom_call" | custom-call | tf_op jit(solution)/shard_map/rounds/pallas_call | solution.py:157
  141.9 8.5 %collective-permute-done.7.first = bf16[2,4,128,128]{3,2,1,0:T(8,128)(2,1)S(1)} collective-permute-done((bf16[2,4,128,128]{3,2,1,0:T(8,128)(2,1)S(1)}, bf16[2,4,128,128]{3,2,1,0:T(8,128)(2,1)S(1)}, u32[]{:S(2)}, u32[]{:S(2)}) %collective-permute-start.7) | collective-permute-done | bytes 262176 | tf_op jit(solution)/shard_map/ppermute | solution.py:226
  150.4 10.7 %collective-permute-done.8.second = bf16[2,4,128,128]{3,2,1,0:T(8,128)(2,1)S(1)} collective-permute-done((bf16[2,4,128,128]{3,2,1,0:T(8,128)(2,1)S(1)}, bf16[2,4,128,128]{3,2,1,0:T(8,128)(2,1)S(1)}, u32[]{:S(2)}, u32[]{:S(2)}) %collective-permute-start.8) | collective-permute-done | bytes 262176 | tf_op jit(solution)/shard_map/ppermute | solution.py:226
  161.2 1.4 place.1
  (8 shorter events, 0.1 us)
Async XLA Ops:
  8.0 113.8 %all-to-all-start = ((bf16[32,8,2,16,128]{4,3,2,1,0:T(8,128)(2,1)}), bf16[32,8,2,16,128]{4,3,2,1,0:T(8,128)(2,1)S(1)}, u32[]{:S(2)}, u32[]{:S(2)}) async-start(bf16[32,8,2,16,128]{4,3,2,1,0:T(8,128)(2,1)} %bitcast.10), calls=%async_computation | async-start | bytes 4194304 | tf_op jit(solution)/shard_map/all_to_all | solution.py:253
  23.6 12.4 %collective-permute-start = (bf16[4,4,2,16,128]{4,3,2,1,0:T(8,128)(2,1)S(1)}, bf16[4,4,2,16,128]{4,3,2,1,0:T(8,128)(2,1)S(1)}, u32[]{:S(2)}, u32[]{:S(2)}) collective-permute-start(bf16[4,4,2,16,128]{4,3,2,1,0:T(8,128)(2,1)S(1)} %get-tuple-element.19), channel_id=1, source_target_pairs={{0,1},{1,0},{2,3},{3,2},{4,5},{5,4},{6,7},{7,6},{8,9},{9,8},{10,11... | collective-permute-start | bytes 393224 | tf_op jit(solution)/shard_map/ppermute | solution.py:234
  26.4 13.9 %collective-permute-start.1 = (bf16[4,4,2,16,128]{4,3,2,1,0:T(8,128)(2,1)S(1)}, bf16[4,4,2,16,128]{4,3,2,1,0:T(8,128)(2,1)S(1)}, u32[]{:S(2)}, u32[]{:S(2)}) collective-permute-start(bf16[4,4,2,16,128]{4,3,2,1,0:T(8,128)(2,1)S(1)} %get-tuple-element.20), channel_id=1, source_target_pairs={{0,2},{1,3},{2,0},{3,1},{4,6},{5,7},{6,4},{7,5},{8,10},{9,11},{10,... | collective-permute-start | bytes 393224 | tf_op jit(solution)/shard_map/ppermute | solution.py:234
  29.1 13.7 %collective-permute-start.2 = (bf16[4,4,2,16,128]{4,3,2,1,0:T(8,128)(2,1)S(1)}, bf16[4,4,2,16,128]{4,3,2,1,0:T(8,128)(2,1)S(1)}, u32[]{:S(2)}, u32[]{:S(2)}) collective-permute-start(bf16[4,4,2,16,128]{4,3,2,1,0:T(8,128)(2,1)S(1)} %get-tuple-element.21), channel_id=1, source_target_pairs={{0,3},{1,2},{2,1},{3,0},{4,7},{5,6},{6,5},{7,4},{8,11},{9,10},{10,... | collective-permute-start | bytes 393224 | tf_op jit(solution)/shard_map/ppermute | solution.py:234
  42.9 65.9 %collective-permute-start.3 = (bf16[4,4,2,16,128]{4,3,2,1,0:T(8,128)(2,1)S(1)}, bf16[4,4,2,16,128]{4,3,2,1,0:T(8,128)(2,1)S(1)}, u32[]{:S(2)}, u32[]{:S(2)}) collective-permute-start(bf16[4,4,2,16,128]{4,3,2,1,0:T(8,128)(2,1)S(1)} %pad_maximum_fusion), channel_id=1, source_target_pairs={{0,96},{1,97},{2,98},{3,99},{4,100},{5,101},{6,102},{7,103},{8,104... | collective-permute-start | bytes 393224 | tf_op jit(solution)/shard_map/ppermute | solution.py:234
  48.7 60.1 %collective-permute-start.4 = (bf16[4,4,2,16,128]{4,3,2,1,0:T(8,128)(2,1)S(1)}, bf16[4,4,2,16,128]{4,3,2,1,0:T(8,128)(2,1)S(1)}, u32[]{:S(2)}, u32[]{:S(2)}) collective-permute-start(bf16[4,4,2,16,128]{4,3,2,1,0:T(8,128)(2,1)S(1)} %pad_maximum_fusion.1), channel_id=1, source_target_pairs={{0,100},{1,101},{2,102},{3,103},{4,96},{5,97},{6,98},{7,99},{8,108... | collective-permute-start | bytes 393224 | tf_op jit(solution)/shard_map/ppermute | solution.py:234
  52.2 56.6 %collective-permute-start.5 = (bf16[4,4,2,16,128]{4,3,2,1,0:T(8,128)(2,1)S(1)}, bf16[4,4,2,16,128]{4,3,2,1,0:T(8,128)(2,1)S(1)}, u32[]{:S(2)}, u32[]{:S(2)}) collective-permute-start(bf16[4,4,2,16,128]{4,3,2,1,0:T(8,128)(2,1)S(1)} %pad_maximum_fusion.2), channel_id=1, source_target_pairs={{0,104},{1,105},{2,106},{3,107},{4,108},{5,109},{6,110},{7,111},{8... | collective-permute-start | bytes 393224 | tf_op jit(solution)/shard_map/ppermute | solution.py:234
  63.0 45.8 %collective-permute-start.6 = (bf16[4,4,2,16,128]{4,3,2,1,0:T(8,128)(2,1)S(1)}, bf16[4,4,2,16,128]{4,3,2,1,0:T(8,128)(2,1)S(1)}, u32[]{:S(2)}, u32[]{:S(2)}) collective-permute-start(bf16[4,4,2,16,128]{4,3,2,1,0:T(8,128)(2,1)S(1)} %pad_maximum_fusion.3), channel_id=1, source_target_pairs={{0,108},{1,109},{2,110},{3,111},{4,104},{5,105},{6,106},{7,107},{8... | collective-permute-start | bytes 393224 | tf_op jit(solution)/shard_map/ppermute | solution.py:234
  121.8 14.9 %collective-permute-start.9 = (bf16[2,16,8,2,16,128]{5,4,3,2,1,0:T(8,128)(2,1)S(1)}, bf16[2,16,8,2,16,128]{5,4,3,2,1,0:T(8,128)(2,1)S(1)}, u32[]{:S(2)}, u32[]{:S(2)}) collective-permute-start(bf16[2,16,8,2,16,128]{5,4,3,2,1,0:T(8,128)(2,1)S(1)} %bitcast.6), channel_id=1, source_target_pairs={{0,16},{16,0},{32,48},{48,32},{64,80},{80,64},{96,112},{112,96},{1... | collective-permute-start | bytes 6291464 | tf_op jit(solution)/shard_map/ppermute | solution.py:226
  124.7 25.7 %collective-permute-start.7 = (bf16[2,4,128,128]{3,2,1,0:T(8,128)(2,1)S(1)}, bf16[2,4,128,128]{3,2,1,0:T(8,128)(2,1)S(1)}, u32[]{:S(2)}, u32[]{:S(2)}) collective-permute-start(bf16[2,4,128,128]{3,2,1,0:T(8,128)(2,1)S(1)} %get-tuple-element.27), channel_id=1, source_target_pairs={{0,32},{16,48},{32,0},{48,16},{64,96},{80,112},{96,64},{112,80},{1... | collective-permute-start | bytes 786440 | tf_op jit(solution)/shard_map/ppermute | solution.py:226
  132.5 28.7 %collective-permute-start.8 = (bf16[2,4,128,128]{3,2,1,0:T(8,128)(2,1)S(1)}, bf16[2,4,128,128]{3,2,1,0:T(8,128)(2,1)S(1)}, u32[]{:S(2)}, u32[]{:S(2)}) collective-permute-start(bf16[2,4,128,128]{3,2,1,0:T(8,128)(2,1)S(1)} %get-tuple-element.28), channel_id=1, source_target_pairs={{0,96},{16,112},{32,64},{48,80},{64,32},{80,48},{96,0},{112,16},{1... | collective-permute-start | bytes 786440 | tf_op jit(solution)/shard_map/ppermute | solution.py:226

commit v5 on v4

--- a/solution.py
+++ b/solution.py
@@ -64,24 +64,17 @@
             slot[:, side * CB : (side + 1) * CB] = ((wide[pl.ds(first, L), :] - mean) * taper[...]).astype(jnp.bfloat16)
         found = jnp.dot(table[...], slot[...], preferred_element_type=jnp.float32)
         for side in range(2):
-            for part in range(2):
-                first_row = part * WD + 2 * pair + side
-                spectra[pl.ds(first_row, K, stride=2 * WD), :] = found[part * K : (part + 1) * K, side * CB : (side + 1) * CB]
-
-    rows = 2 * KL * WD
-
-    def add(f, power):
-        part = spectra[pl.ds(pl.multiple_of(f * rows, rows), rows), :].reshape(2 * KL, WD, CB)
-        return power + jnp.sum(part * part, axis=0)
-
-    power = lax.fori_loop(0, NF, add, jnp.zeros((WD, CB), jnp.float32), unroll=4)
+            spectra[2 * pair + side] = found[:, side * CB : (side + 1) * CB]
+
+    power = jnp.concatenate([jnp.sum(spectra[w] * spectra[w], axis=0, keepdims=True) for w in range(WD)], axis=0)
     gain = lax.rsqrt(power * (1.0 / (2 * K)) + 1e-6)[None]
 
     def whiten(f, carry):
-        for h in range(2):
-            first = pl.multiple_of(f * rows + (position[0] ^ h) * (rows // 2), rows // 2)
-            part = spectra[pl.ds(first, rows // 2), :].reshape(KL, WD, CB)
-            ready[f, h * HB : (h + 1) * HB] = (part * gain).astype(jnp.bfloat16).reshape(HB, 2, WD, CB)
+        for e in range(2):
+            part = spectra[:, pl.ds(pl.multiple_of(e * K + f * KL, KL), KL), :]
+            part = (jnp.swapaxes(part, 0, 1) * gain).astype(jnp.bfloat16)
+            for h in range(2):
+                ready[f, pl.ds((position[0] ^ h) * HB, HB), e] = part[h * HB : (h + 1) * HB]
         for number in range(2):
             pltpu.make_async_copy(ready.at[f], white.at[number, f], out_sems.at[number]).start()
         return carry
@@ -114,7 +107,7 @@
             pltpu.VMEM((L, CB), jnp.float32),
             pltpu.VMEM((2 * K, L), jnp.bfloat16),
             pltpu.VMEM((2, L, 2 * CB), jnp.bfloat16),
-            pltpu.VMEM((2 * K * WD + 2 * WD, CB), jnp.float32),
+            pltpu.VMEM((WD, 2 * K, CB), jnp.float32),
             pltpu.VMEM((NF, KL, 2, WD, CB), jnp.bfloat16),
             pltpu.SemaphoreType.DMA((3,)),
             pltpu.SemaphoreType.DMA((2,)),

time: 163 us -> 162 us (level)
  no operation moved by 1% of the time
where the time goes in v5:
time: 162 us; the launch traced here: 161 us
  waiting for transfers between devices  84.9 us (52%)
  starting transfers between devices  61.8 us (38%)
  Pallas kernels  14.4 us (9%)
    ppermute x7, waiting for transfers between devices, send(): return lax.ppermute(block, ('chan', 'freq'), moves)  52.7 us
    ppermute x7, starting transfers between devices, send(): return lax.ppermute(block, ('chan', 'freq'), moves)  32.3 us
    ppermute x3, waiting for transfers between devices, partner(): return lax.ppermute(block, 'chan', [(i, i ^ mask) for i in range(count)])  19.2 us
    all_to_all x1, starting transfers between devices, per_device(): lax.all_to_all(white.reshape((2 * NF,) + white.shape[2:]), ('chan', 'freq...  15.6 us
    ppermute x3, starting transfers between devices, partner(): return lax.ppermute(block, 'chan', [(i, i ^ mask) for i in range(count)])  13.9 us
    all_to_all x1, waiting for transfers between devices, per_device(): lax.all_to_all(white.reshape((2 * NF,) + white.shape[2:]), ('chan', 'freq...  13 us
    pallas_call x1, Pallas kernels, front(): pl.pallas_call(front_kernel, out_shape=(pltpu.HBM((2, NF, KL, 2, WD, CB),...  6.84 us
    pallas_call x1, Pallas kernels, rounds(): pl.pallas_call(rounds_kernel, out_shape=jax.ShapeDtypeStruct((ROUNDS, 2,...  5.19 us
  transfers between devices with their start and end apart: 11, of which 7 were waited for; matrix products, arithmetic and copies ran while one was open for 0% of the time, Pallas kernels for 4%

profile of v5, /device:TPU:6, one launch (start us, length us, event | category | flops | bytes accessed | tf_op | source)
XLA Modules:
  0.0 161.5 jit_solution(11720924379780876017)
XLA Ops:
  0.0 0.1 pad_add_fusion.position
  0.1 6.8 %white.1 = (bf16[2,16,8,2,16,128]{5,4,3,2,1,0:T(8,128)(2,1)}, bf16[4,4,2,16,128]{4,3,2,1,0:T(8,128)(2,1)S(1)}, bf16[4,4,2,16,128]{4,3,2,1,0:T(8,128)(2,1)S(1)}, ...) custom-call(s32[3]{0:T(128)S(1)} %pad_add_fusion.position, s32[16]{0:T(128)} %starts_in.1, ...), custom_call_target="tpu_custom_call" | custom-call | tf_op jit(solution)/shard_map/white/pallas_call | solution.py:96
  6.9 15.6 %all-to-all-start = ((bf16[32,8,2,16,128]{4,3,2,1,0:T(8,128)(2,1)}), bf16[32,8,2,16,128]{4,3,2,1,0:T(8,128)(2,1)S(1)}, u32[]{:S(2)}, u32[]{:S(2)}) async-start(bf16[32,8,2,16,128]{4,3,2,1,0:T(8,128)(2,1)} %bitcast.10), calls=%async_computation | async-start | bytes 4194304 | tf_op jit(solution)/shard_map/all_to_all | solution.py:246
  22.5 2.8 %collective-permute-start = (bf16[4,4,2,16,128]{4,3,2,1,0:T(8,128)(2,1)S(1)}, bf16[4,4,2,16,128]{4,3,2,1,0:T(8,128)(2,1)S(1)}, u32[]{:S(2)}, u32[]{:S(2)}) collective-permute-start(bf16[4,4,2,16,128]{4,3,2,1,0:T(8,128)(2,1)S(1)} %get-tuple-element.19), channel_id=1, source_target_pairs={{0,1},{1,0},{2,3},{3,2},{4,5},{5,4},{6,7},{7,6},{8,9},{9,8},{10,11... | collective-permute-start | bytes 393224 | tf_op jit(solution)/shard_map/ppermute | solution.py:227
  25.3 2.7 %collective-permute-start.1 = (bf16[4,4,2,16,128]{4,3,2,1,0:T(8,128)(2,1)S(1)}, bf16[4,4,2,16,128]{4,3,2,1,0:T(8,128)(2,1)S(1)}, u32[]{:S(2)}, u32[]{:S(2)}) collective-permute-start(bf16[4,4,2,16,128]{4,3,2,1,0:T(8,128)(2,1)S(1)} %get-tuple-element.20), channel_id=1, source_target_pairs={{0,2},{1,3},{2,0},{3,1},{4,6},{5,7},{6,4},{7,5},{8,10},{9,11},{10,... | collective-permute-start | bytes 393224 | tf_op jit(solution)/shard_map/ppermute | solution.py:227
  28.0 4.9 %collective-permute-start.2 = (bf16[4,4,2,16,128]{4,3,2,1,0:T(8,128)(2,1)S(1)}, bf16[4,4,2,16,128]{4,3,2,1,0:T(8,128)(2,1)S(1)}, u32[]{:S(2)}, u32[]{:S(2)}) collective-permute-start(bf16[4,4,2,16,128]{4,3,2,1,0:T(8,128)(2,1)S(1)} %get-tuple-element.21), channel_id=1, source_target_pairs={{0,3},{1,2},{2,1},{3,0},{4,7},{5,6},{6,5},{7,4},{8,11},{9,10},{10,... | collective-permute-start | bytes 393224 | tf_op jit(solution)/shard_map/ppermute | solution.py:227
  33.0 1.9 %collective-permute-done = bf16[4,4,2,16,128]{4,3,2,1,0:T(8,128)(2,1)S(1)} collective-permute-done((bf16[4,4,2,16,128]{4,3,2,1,0:T(8,128)(2,1)S(1)}, bf16[4,4,2,16,128]{4,3,2,1,0:T(8,128)(2,1)S(1)}, u32[]{:S(2)}, u32[]{:S(2)}) %collective-permute-start) | collective-permute-done | bytes 131104 | tf_op jit(solution)/shard_map/ppermute | solution.py:227
  34.9 4.3 %collective-permute-done.1 = bf16[4,4,2,16,128]{4,3,2,1,0:T(8,128)(2,1)S(1)} collective-permute-done((bf16[4,4,2,16,128]{4,3,2,1,0:T(8,128)(2,1)S(1)}, bf16[4,4,2,16,128]{4,3,2,1,0:T(8,128)(2,1)S(1)}, u32[]{:S(2)}, u32[]{:S(2)}) %collective-permute-start.1) | collective-permute-done | bytes 131104 | tf_op jit(solution)/shard_map/ppermute | solution.py:227
  39.2 2.6 %collective-permute-done.2 = bf16[4,4,2,16,128]{4,3,2,1,0:T(8,128)(2,1)S(1)} collective-permute-done((bf16[4,4,2,16,128]{4,3,2,1,0:T(8,128)(2,1)S(1)}, bf16[4,4,2,16,128]{4,3,2,1,0:T(8,128)(2,1)S(1)}, u32[]{:S(2)}, u32[]{:S(2)}) %collective-permute-start.2) | collective-permute-done | bytes 131104 | tf_op jit(solution)/shard_map/ppermute | solution.py:227
  41.8 5.7 %collective-permute-start.3 = (bf16[4,4,2,16,128]{4,3,2,1,0:T(8,128)(2,1)S(1)}, bf16[4,4,2,16,128]{4,3,2,1,0:T(8,128)(2,1)S(1)}, u32[]{:S(2)}, u32[]{:S(2)}) collective-permute-start(bf16[4,4,2,16,128]{4,3,2,1,0:T(8,128)(2,1)S(1)} %pad_maximum_fusion), channel_id=1, source_target_pairs={{0,96},{1,97},{2,98},{3,99},{4,100},{5,101},{6,102},{7,103},{8,104... | collective-permute-start | bytes 393224 | tf_op jit(solution)/shard_map/ppermute | solution.py:227
  47.6 3.5 %collective-permute-start.4 = (bf16[4,4,2,16,128]{4,3,2,1,0:T(8,128)(2,1)S(1)}, bf16[4,4,2,16,128]{4,3,2,1,0:T(8,128)(2,1)S(1)}, u32[]{:S(2)}, u32[]{:S(2)}) collective-permute-start(bf16[4,4,2,16,128]{4,3,2,1,0:T(8,128)(2,1)S(1)} %pad_maximum_fusion.1), channel_id=1, source_target_pairs={{0,100},{1,101},{2,102},{3,103},{4,96},{5,97},{6,98},{7,99},{8,108... | collective-permute-start | bytes 393224 | tf_op jit(solution)/shard_map/ppermute | solution.py:227
  51.1 10.7 %collective-permute-start.5 = (bf16[4,4,2,16,128]{4,3,2,1,0:T(8,128)(2,1)S(1)}, bf16[4,4,2,16,128]{4,3,2,1,0:T(8,128)(2,1)S(1)}, u32[]{:S(2)}, u32[]{:S(2)}) collective-permute-start(bf16[4,4,2,16,128]{4,3,2,1,0:T(8,128)(2,1)S(1)} %pad_maximum_fusion.2), channel_id=1, source_target_pairs={{0,104},{1,105},{2,106},{3,107},{4,108},{5,109},{6,110},{7,111},{8... | collective-permute-start | bytes 393224 | tf_op jit(solution)/shard_map/ppermute | solution.py:227
  61.9 1.9 %collective-permute-start.6 = (bf16[4,4,2,16,128]{4,3,2,1,0:T(8,128)(2,1)S(1)}, bf16[4,4,2,16,128]{4,3,2,1,0:T(8,128)(2,1)S(1)}, u32[]{:S(2)}, u32[]{:S(2)}) collective-permute-start(bf16[4,4,2,16,128]{4,3,2,1,0:T(8,128)(2,1)S(1)} %pad_maximum_fusion.3), channel_id=1, source_target_pairs={{0,108},{1,109},{2,110},{3,111},{4,104},{5,105},{6,106},{7,107},{8... | collective-permute-start | bytes 393224 | tf_op jit(solution)/shard_map/ppermute | solution.py:227
  63.8 43.9 %collective-permute-done.3.refs_0_ = bf16[4,4,2,16,128]{4,3,2,1,0:T(8,128)(2,1)S(1)} collective-permute-done((bf16[4,4,2,16,128]{4,3,2,1,0:T(8,128)(2,1)S(1)}, bf16[4,4,2,16,128]{4,3,2,1,0:T(8,128)(2,1)S(1)}, u32[]{:S(2)}, u32[]{:S(2)}) %collective-permute-start.3) | collective-permute-done | bytes 131104 | tf_op jit(solution)/shard_map/ppermute | solution.py:227
  107.7 0.0 collective-permute-done.4.refs_1_
  107.7 0.0 collective-permute-done.5.refs_2_
  107.7 0.0 collective-permute-done.6.refs_3_
  107.8 13.0 %all-to-all-done = bf16[32,8,2,16,128]{4,3,2,1,0:T(8,128)(2,1)S(1)} async-done(((bf16[32,8,2,16,128]{4,3,2,1,0:T(8,128)(2,1)}), bf16[32,8,2,16,128]{4,3,2,1,0:T(8,128)(2,1)S(1)}, u32[]{:S(2)}, u32[]{:S(2)}) %all-to-all-start) | async-done | bytes 2097184 | tf_op jit(solution)/shard_map/all_to_all | solution.py:246
  120.7 1.9 %collective-permute-start.9 = (bf16[2,16,8,2,16,128]{5,4,3,2,1,0:T(8,128)(2,1)S(1)}, bf16[2,16,8,2,16,128]{5,4,3,2,1,0:T(8,128)(2,1)S(1)}, u32[]{:S(2)}, u32[]{:S(2)}) collective-permute-start(bf16[2,16,8,2,16,128]{5,4,3,2,1,0:T(8,128)(2,1)S(1)} %bitcast.6), channel_id=1, source_target_pairs={{0,16},{16,0},{32,48},{48,32},{64,80},{80,64},{96,112},{112,96},{1... | collective-permute-start | bytes 6291464 | tf_op jit(solution)/shard_map/ppermute | solution.py:219
  122.7 1.0 between.1
  123.6 7.8 %collective-permute-start.7 = (bf16[2,4,128,128]{3,2,1,0:T(8,128)(2,1)S(1)}, bf16[2,4,128,128]{3,2,1,0:T(8,128)(2,1)S(1)}, u32[]{:S(2)}, u32[]{:S(2)}) collective-permute-start(bf16[2,4,128,128]{3,2,1,0:T(8,128)(2,1)S(1)} %get-tuple-element.27), channel_id=1, source_target_pairs={{0,32},{16,48},{32,0},{48,16},{64,96},{80,112},{96,64},{112,80},{1... | collective-permute-start | bytes 786440 | tf_op jit(solution)/shard_map/ppermute | solution.py:219
  131.4 4.3 %collective-permute-start.8 = (bf16[2,4,128,128]{3,2,1,0:T(8,128)(2,1)S(1)}, bf16[2,4,128,128]{3,2,1,0:T(8,128)(2,1)S(1)}, u32[]{:S(2)}, u32[]{:S(2)}) collective-permute-start(bf16[2,4,128,128]{3,2,1,0:T(8,128)(2,1)S(1)} %get-tuple-element.28), channel_id=1, source_target_pairs={{0,96},{16,112},{32,64},{48,80},{64,32},{80,48},{96,0},{112,16},{1... | collective-permute-start | bytes 786440 | tf_op jit(solution)/shard_map/ppermute | solution.py:219
  135.7 0.0 collective-permute-done.9.own_swapped.far_swapped
  135.7 5.2 %rounds.1.base = bf16[4,2,8,128,128]{4,3,2,1,0:T(8,128)(2,1)} custom-call(s32[3]{0:T(128)S(1)} %pad_add_fusion.position, bf16[2,16,8,2,16,128]{5,4,3,2,1,0:T(8,128)(2,1)S(1)} %bitcast.8, bf16[2,16,8,2,16,128]{5,4,3,2,1,0:T(8,128)(2,1)S(1)} %bitcast.9, bf16[2,16,8,2,16,128]{5,4,3,2,1,0:T(8,128)(2,1)S(1)} %collective-permute-done.9.own_swapped.far_swapped, ...), custom_call_target="tpu_custom_call" | custom-call | tf_op jit(solution)/shard_map/rounds/pallas_call | solution.py:150
  140.9 8.5 %collective-permute-done.7.first = bf16[2,4,128,128]{3,2,1,0:T(8,128)(2,1)S(1)} collective-permute-done((bf16[2,4,128,128]{3,2,1,0:T(8,128)(2,1)S(1)}, bf16[2,4,128,128]{3,2,1,0:T(8,128)(2,1)S(1)}, u32[]{:S(2)}, u32[]{:S(2)}) %collective-permute-start.7) | collective-permute-done | bytes 262176 | tf_op jit(solution)/shard_map/ppermute | solution.py:219
  149.4 10.7 %collective-permute-done.8.second = bf16[2,4,128,128]{3,2,1,0:T(8,128)(2,1)S(1)} collective-permute-done((bf16[2,4,128,128]{3,2,1,0:T(8,128)(2,1)S(1)}, bf16[2,4,128,128]{3,2,1,0:T(8,128)(2,1)S(1)}, u32[]{:S(2)}, u32[]{:S(2)}) %collective-permute-start.8) | collective-permute-done | bytes 262176 | tf_op jit(solution)/shard_map/ppermute | solution.py:219
  160.1 1.4 place.1
  (8 shorter events, 0.1 us)
Async XLA Ops:
  6.9 113.8 %all-to-all-start = ((bf16[32,8,2,16,128]{4,3,2,1,0:T(8,128)(2,1)}), bf16[32,8,2,16,128]{4,3,2,1,0:T(8,128)(2,1)S(1)}, u32[]{:S(2)}, u32[]{:S(2)}) async-start(bf16[32,8,2,16,128]{4,3,2,1,0:T(8,128)(2,1)} %bitcast.10), calls=%async_computation | async-start | bytes 4194304 | tf_op jit(solution)/shard_map/all_to_all | solution.py:246
  22.5 12.4 %collective-permute-start = (bf16[4,4,2,16,128]{4,3,2,1,0:T(8,128)(2,1)S(1)}, bf16[4,4,2,16,128]{4,3,2,1,0:T(8,128)(2,1)S(1)}, u32[]{:S(2)}, u32[]{:S(2)}) collective-permute-start(bf16[4,4,2,16,128]{4,3,2,1,0:T(8,128)(2,1)S(1)} %get-tuple-element.19), channel_id=1, source_target_pairs={{0,1},{1,0},{2,3},{3,2},{4,5},{5,4},{6,7},{7,6},{8,9},{9,8},{10,11... | collective-permute-start | bytes 393224 | tf_op jit(solution)/shard_map/ppermute | solution.py:227
  25.3 13.9 %collective-permute-start.1 = (bf16[4,4,2,16,128]{4,3,2,1,0:T(8,128)(2,1)S(1)}, bf16[4,4,2,16,128]{4,3,2,1,0:T(8,128)(2,1)S(1)}, u32[]{:S(2)}, u32[]{:S(2)}) collective-permute-start(bf16[4,4,2,16,128]{4,3,2,1,0:T(8,128)(2,1)S(1)} %get-tuple-element.20), channel_id=1, source_target_pairs={{0,2},{1,3},{2,0},{3,1},{4,6},{5,7},{6,4},{7,5},{8,10},{9,11},{10,... | collective-permute-start | bytes 393224 | tf_op jit(solution)/shard_map/ppermute | solution.py:227
  28.0 13.8 %collective-permute-start.2 = (bf16[4,4,2,16,128]{4,3,2,1,0:T(8,128)(2,1)S(1)}, bf16[4,4,2,16,128]{4,3,2,1,0:T(8,128)(2,1)S(1)}, u32[]{:S(2)}, u32[]{:S(2)}) collective-permute-start(bf16[4,4,2,16,128]{4,3,2,1,0:T(8,128)(2,1)S(1)} %get-tuple-element.21), channel_id=1, source_target_pairs={{0,3},{1,2},{2,1},{3,0},{4,7},{5,6},{6,5},{7,4},{8,11},{9,10},{10,... | collective-permute-start | bytes 393224 | tf_op jit(solution)/shard_map/ppermute | solution.py:227
  41.8 65.9 %collective-permute-start.3 = (bf16[4,4,2,16,128]{4,3,2,1,0:T(8,128)(2,1)S(1)}, bf16[4,4,2,16,128]{4,3,2,1,0:T(8,128)(2,1)S(1)}, u32[]{:S(2)}, u32[]{:S(2)}) collective-permute-start(bf16[4,4,2,16,128]{4,3,2,1,0:T(8,128)(2,1)S(1)} %pad_maximum_fusion), channel_id=1, source_target_pairs={{0,96},{1,97},{2,98},{3,99},{4,100},{5,101},{6,102},{7,103},{8,104... | collective-permute-start | bytes 393224 | tf_op jit(solution)/shard_map/ppermute | solution.py:227
  47.6 60.2 %collective-permute-start.4 = (bf16[4,4,2,16,128]{4,3,2,1,0:T(8,128)(2,1)S(1)}, bf16[4,4,2,16,128]{4,3,2,1,0:T(8,128)(2,1)S(1)}, u32[]{:S(2)}, u32[]{:S(2)}) collective-permute-start(bf16[4,4,2,16,128]{4,3,2,1,0:T(8,128)(2,1)S(1)} %pad_maximum_fusion.1), channel_id=1, source_target_pairs={{0,100},{1,101},{2,102},{3,103},{4,96},{5,97},{6,98},{7,99},{8,108... | collective-permute-start | bytes 393224 | tf_op jit(solution)/shard_map/ppermute | solution.py:227
  51.1 56.6 %collective-permute-start.5 = (bf16[4,4,2,16,128]{4,3,2,1,0:T(8,128)(2,1)S(1)}, bf16[4,4,2,16,128]{4,3,2,1,0:T(8,128)(2,1)S(1)}, u32[]{:S(2)}, u32[]{:S(2)}) collective-permute-start(bf16[4,4,2,16,128]{4,3,2,1,0:T(8,128)(2,1)S(1)} %pad_maximum_fusion.2), channel_id=1, source_target_pairs={{0,104},{1,105},{2,106},{3,107},{4,108},{5,109},{6,110},{7,111},{8... | collective-permute-start | bytes 393224 | tf_op jit(solution)/shard_map/ppermute | solution.py:227
  61.9 45.9 %collective-permute-start.6 = (bf16[4,4,2,16,128]{4,3,2,1,0:T(8,128)(2,1)S(1)}, bf16[4,4,2,16,128]{4,3,2,1,0:T(8,128)(2,1)S(1)}, u32[]{:S(2)}, u32[]{:S(2)}) collective-permute-start(bf16[4,4,2,16,128]{4,3,2,1,0:T(8,128)(2,1)S(1)} %pad_maximum_fusion.3), channel_id=1, source_target_pairs={{0,108},{1,109},{2,110},{3,111},{4,104},{5,105},{6,106},{7,107},{8... | collective-permute-start | bytes 393224 | tf_op jit(solution)/shard_map/ppermute | solution.py:227
  120.7 14.9 %collective-permute-start.9 = (bf16[2,16,8,2,16,128]{5,4,3,2,1,0:T(8,128)(2,1)S(1)}, bf16[2,16,8,2,16,128]{5,4,3,2,1,0:T(8,128)(2,1)S(1)}, u32[]{:S(2)}, u32[]{:S(2)}) collective-permute-start(bf16[2,16,8,2,16,128]{5,4,3,2,1,0:T(8,128)(2,1)S(1)} %bitcast.6), channel_id=1, source_target_pairs={{0,16},{16,0},{32,48},{48,32},{64,80},{80,64},{96,112},{112,96},{1... | collective-permute-start | bytes 6291464 | tf_op jit(solution)/shard_map/ppermute | solution.py:219
  123.6 25.8 %collective-permute-start.7 = (bf16[2,4,128,128]{3,2,1,0:T(8,128)(2,1)S(1)}, bf16[2,4,128,128]{3,2,1,0:T(8,128)(2,1)S(1)}, u32[]{:S(2)}, u32[]{:S(2)}) collective-permute-start(bf16[2,4,128,128]{3,2,1,0:T(8,128)(2,1)S(1)} %get-tuple-element.27), channel_id=1, source_target_pairs={{0,32},{16,48},{32,0},{48,16},{64,96},{80,112},{96,64},{112,80},{1... | collective-permute-start | bytes 786440 | tf_op jit(solution)/shard_map/ppermute | solution.py:219
  131.4 28.7 %collective-permute-start.8 = (bf16[2,4,128,128]{3,2,1,0:T(8,128)(2,1)S(1)}, bf16[2,4,128,128]{3,2,1,0:T(8,128)(2,1)S(1)}, u32[]{:S(2)}, u32[]{:S(2)}) collective-permute-start(bf16[2,4,128,128]{3,2,1,0:T(8,128)(2,1)S(1)} %get-tuple-element.28), channel_id=1, source_target_pairs={{0,96},{16,112},{32,64},{48,80},{64,32},{80,48},{96,0},{112,16},{1... | collective-permute-start | bytes 786440 | tf_op jit(solution)/shard_map/ppermute | solution.py:219

commit v6 on v5

--- a/solution.py
+++ b/solution.py
@@ -56,6 +56,7 @@
     copies[2].wait()
     wide[:SEG, :] = held[...].astype(jnp.float32)
     wide[SEG:, :] = jnp.zeros((2 * WD, CB), jnp.float32)
+    power = []
     for pair in range(WD // 2):
         slot = tapered.at[pair % 2]
         for side in range(2):
@@ -65,9 +66,10 @@
         found = jnp.dot(table[...], slot[...], preferred_element_type=jnp.float32)
         for side in range(2):
             spectra[2 * pair + side] = found[:, side * CB : (side + 1) * CB]
-
-    power = jnp.concatenate([jnp.sum(spectra[w] * spectra[w], axis=0, keepdims=True) for w in range(WD)], axis=0)
-    gain = lax.rsqrt(power * (1.0 / (2 * K)) + 1e-6)[None]
+        squares = jnp.sum(found * found, axis=0, keepdims=True)
+        power += [squares[:, :CB], squares[:, CB:]]
+
+    gain = lax.rsqrt(jnp.concatenate(power, axis=0) * (1.0 / (2 * K)) + 1e-6)[None]
 
     def whiten(f, carry):
         for e in range(2):
@@ -79,7 +81,7 @@
             pltpu.make_async_copy(ready.at[f], white.at[number, f], out_sems.at[number]).start()
         return carry
 
-    lax.fori_loop(0, NF, whiten, 0, unroll=4)
+    lax.fori_loop(0, NF, whiten, 0)
     for e, out in enumerate(crossed):
         for d in range(NZ):
             out[d] = ready[(d * NX + e) ^ position[1], HB:]

time: 162 us -> 162 us (level)
  no operation moved by 1% of the time
where the time goes in v6:
time: 162 us
  waiting for transfers between devices  84.9 us (52%)
  starting transfers between devices  61.9 us (38%)
  Pallas kernels  14.3 us (9%)
    ppermute x7, waiting for transfers between devices, send(): return lax.ppermute(block, ('chan', 'freq'), moves)  52.7 us
    ppermute x7, starting transfers between devices, send(): return lax.ppermute(block, ('chan', 'freq'), moves)  32.3 us
    ppermute x3, waiting for transfers between devices, partner(): return lax.ppermute(block, 'chan', [(i, i ^ mask) for i in range(count)])  19.2 us
    all_to_all x1, starting transfers between devices, per_device(): lax.all_to_all(white.reshape((2 * NF,) + white.shape[2:]), ('chan', 'freq...  15.7 us
    ppermute x3, starting transfers between devices, partner(): return lax.ppermute(block, 'chan', [(i, i ^ mask) for i in range(count)])  13.9 us
    all_to_all x1, waiting for transfers between devices, per_device(): lax.all_to_all(white.reshape((2 * NF,) + white.shape[2:]), ('chan', 'freq...  13 us
    pallas_call x1, Pallas kernels, front(): pl.pallas_call(front_kernel, out_shape=(pltpu.HBM((2, NF, KL, 2, WD, CB),...  6.79 us
    pallas_call x1, Pallas kernels, rounds(): pl.pallas_call(rounds_kernel, out_shape=jax.ShapeDtypeStruct((ROUNDS, 2,...  5.19 us
  transfers between devices with their start and end apart: 11, of which 7 were waited for; matrix products, arithmetic and copies ran while one was open for 0% of the time, Pallas kernels for 4%

profile of v6, /device:TPU:6, one launch (start us, length us, event | category | flops | bytes accessed | tf_op | source)
XLA Modules:
  0.0 161.5 jit_solution(12689943357568797941)
XLA Ops:
  0.0 0.1 pad_add_fusion.position
  0.1 6.8 %white.1 = (bf16[2,16,8,2,16,128]{5,4,3,2,1,0:T(8,128)(2,1)}, bf16[4,4,2,16,128]{4,3,2,1,0:T(8,128)(2,1)S(1)}, bf16[4,4,2,16,128]{4,3,2,1,0:T(8,128)(2,1)S(1)}, ...) custom-call(s32[3]{0:T(128)S(1)} %pad_add_fusion.position, s32[16]{0:T(128)} %starts_in.1, ...), custom_call_target="tpu_custom_call" | custom-call | tf_op jit(solution)/shard_map/white/pallas_call | solution.py:98
  6.9 15.7 %all-to-all-start = ((bf16[32,8,2,16,128]{4,3,2,1,0:T(8,128)(2,1)}), bf16[32,8,2,16,128]{4,3,2,1,0:T(8,128)(2,1)S(1)}, u32[]{:S(2)}, u32[]{:S(2)}) async-start(bf16[32,8,2,16,128]{4,3,2,1,0:T(8,128)(2,1)} %bitcast.10), calls=%async_computation | async-start | bytes 4194304 | tf_op jit(solution)/shard_map/all_to_all | solution.py:248
  22.5 2.8 %collective-permute-start = (bf16[4,4,2,16,128]{4,3,2,1,0:T(8,128)(2,1)S(1)}, bf16[4,4,2,16,128]{4,3,2,1,0:T(8,128)(2,1)S(1)}, u32[]{:S(2)}, u32[]{:S(2)}) collective-permute-start(bf16[4,4,2,16,128]{4,3,2,1,0:T(8,128)(2,1)S(1)} %get-tuple-element.19), channel_id=1, source_target_pairs={{0,1},{1,0},{2,3},{3,2},{4,5},{5,4},{6,7},{7,6},{8,9},{9,8},{10,11... | collective-permute-start | bytes 393224 | tf_op jit(solution)/shard_map/ppermute | solution.py:229
  25.3 2.7 %collective-permute-start.1 = (bf16[4,4,2,16,128]{4,3,2,1,0:T(8,128)(2,1)S(1)}, bf16[4,4,2,16,128]{4,3,2,1,0:T(8,128)(2,1)S(1)}, u32[]{:S(2)}, u32[]{:S(2)}) collective-permute-start(bf16[4,4,2,16,128]{4,3,2,1,0:T(8,128)(2,1)S(1)} %get-tuple-element.20), channel_id=1, source_target_pairs={{0,2},{1,3},{2,0},{3,1},{4,6},{5,7},{6,4},{7,5},{8,10},{9,11},{10,... | collective-permute-start | bytes 393224 | tf_op jit(solution)/shard_map/ppermute | solution.py:229
  28.1 4.9 %collective-permute-start.2 = (bf16[4,4,2,16,128]{4,3,2,1,0:T(8,128)(2,1)S(1)}, bf16[4,4,2,16,128]{4,3,2,1,0:T(8,128)(2,1)S(1)}, u32[]{:S(2)}, u32[]{:S(2)}) collective-permute-start(bf16[4,4,2,16,128]{4,3,2,1,0:T(8,128)(2,1)S(1)} %get-tuple-element.21), channel_id=1, source_target_pairs={{0,3},{1,2},{2,1},{3,0},{4,7},{5,6},{6,5},{7,4},{8,11},{9,10},{10,... | collective-permute-start | bytes 393224 | tf_op jit(solution)/shard_map/ppermute | solution.py:229
  33.0 1.9 %collective-permute-done = bf16[4,4,2,16,128]{4,3,2,1,0:T(8,128)(2,1)S(1)} collective-permute-done((bf16[4,4,2,16,128]{4,3,2,1,0:T(8,128)(2,1)S(1)}, bf16[4,4,2,16,128]{4,3,2,1,0:T(8,128)(2,1)S(1)}, u32[]{:S(2)}, u32[]{:S(2)}) %collective-permute-start) | collective-permute-done | bytes 131104 | tf_op jit(solution)/shard_map/ppermute | solution.py:229
  34.9 4.3 %collective-permute-done.1 = bf16[4,4,2,16,128]{4,3,2,1,0:T(8,128)(2,1)S(1)} collective-permute-done((bf16[4,4,2,16,128]{4,3,2,1,0:T(8,128)(2,1)S(1)}, bf16[4,4,2,16,128]{4,3,2,1,0:T(8,128)(2,1)S(1)}, u32[]{:S(2)}, u32[]{:S(2)}) %collective-permute-start.1) | collective-permute-done | bytes 131104 | tf_op jit(solution)/shard_map/ppermute | solution.py:229
  39.2 2.6 %collective-permute-done.2 = bf16[4,4,2,16,128]{4,3,2,1,0:T(8,128)(2,1)S(1)} collective-permute-done((bf16[4,4,2,16,128]{4,3,2,1,0:T(8,128)(2,1)S(1)}, bf16[4,4,2,16,128]{4,3,2,1,0:T(8,128)(2,1)S(1)}, u32[]{:S(2)}, u32[]{:S(2)}) %collective-permute-start.2) | collective-permute-done | bytes 131104 | tf_op jit(solution)/shard_map/ppermute | solution.py:229
  41.9 5.7 %collective-permute-start.3 = (bf16[4,4,2,16,128]{4,3,2,1,0:T(8,128)(2,1)S(1)}, bf16[4,4,2,16,128]{4,3,2,1,0:T(8,128)(2,1)S(1)}, u32[]{:S(2)}, u32[]{:S(2)}) collective-permute-start(bf16[4,4,2,16,128]{4,3,2,1,0:T(8,128)(2,1)S(1)} %pad_maximum_fusion), channel_id=1, source_target_pairs={{0,96},{1,97},{2,98},{3,99},{4,100},{5,101},{6,102},{7,103},{8,104... | collective-permute-start | bytes 393224 | tf_op jit(solution)/shard_map/ppermute | solution.py:229
  47.6 3.5 %collective-permute-start.4 = (bf16[4,4,2,16,128]{4,3,2,1,0:T(8,128)(2,1)S(1)}, bf16[4,4,2,16,128]{4,3,2,1,0:T(8,128)(2,1)S(1)}, u32[]{:S(2)}, u32[]{:S(2)}) collective-permute-start(bf16[4,4,2,16,128]{4,3,2,1,0:T(8,128)(2,1)S(1)} %pad_maximum_fusion.1), channel_id=1, source_target_pairs={{0,100},{1,101},{2,102},{3,103},{4,96},{5,97},{6,98},{7,99},{8,108... | collective-permute-start | bytes 393224 | tf_op jit(solution)/shard_map/ppermute | solution.py:229
  51.1 10.8 %collective-permute-start.5 = (bf16[4,4,2,16,128]{4,3,2,1,0:T(8,128)(2,1)S(1)}, bf16[4,4,2,16,128]{4,3,2,1,0:T(8,128)(2,1)S(1)}, u32[]{:S(2)}, u32[]{:S(2)}) collective-permute-start(bf16[4,4,2,16,128]{4,3,2,1,0:T(8,128)(2,1)S(1)} %pad_maximum_fusion.2), channel_id=1, source_target_pairs={{0,104},{1,105},{2,106},{3,107},{4,108},{5,109},{6,110},{7,111},{8... | collective-permute-start | bytes 393224 | tf_op jit(solution)/shard_map/ppermute | solution.py:229
  61.9 1.9 %collective-permute-start.6 = (bf16[4,4,2,16,128]{4,3,2,1,0:T(8,128)(2,1)S(1)}, bf16[4,4,2,16,128]{4,3,2,1,0:T(8,128)(2,1)S(1)}, u32[]{:S(2)}, u32[]{:S(2)}) collective-permute-start(bf16[4,4,2,16,128]{4,3,2,1,0:T(8,128)(2,1)S(1)} %pad_maximum_fusion.3), channel_id=1, source_target_pairs={{0,108},{1,109},{2,110},{3,111},{4,104},{5,105},{6,106},{7,107},{8... | collective-permute-start | bytes 393224 | tf_op jit(solution)/shard_map/ppermute | solution.py:229
  63.9 43.9 %collective-permute-done.3.refs_0_ = bf16[4,4,2,16,128]{4,3,2,1,0:T(8,128)(2,1)S(1)} collective-permute-done((bf16[4,4,2,16,128]{4,3,2,1,0:T(8,128)(2,1)S(1)}, bf16[4,4,2,16,128]{4,3,2,1,0:T(8,128)(2,1)S(1)}, u32[]{:S(2)}, u32[]{:S(2)}) %collective-permute-start.3) | collective-permute-done | bytes 131104 | tf_op jit(solution)/shard_map/ppermute | solution.py:229
  107.8 0.0 collective-permute-done.4.refs_1_
  107.8 0.0 collective-permute-done.5.refs_2_
  107.8 0.0 collective-permute-done.6.refs_3_
  107.8 13.0 %all-to-all-done = bf16[32,8,2,16,128]{4,3,2,1,0:T(8,128)(2,1)S(1)} async-done(((bf16[32,8,2,16,128]{4,3,2,1,0:T(8,128)(2,1)}), bf16[32,8,2,16,128]{4,3,2,1,0:T(8,128)(2,1)S(1)}, u32[]{:S(2)}, u32[]{:S(2)}) %all-to-all-start) | async-done | bytes 2097184 | tf_op jit(solution)/shard_map/all_to_all | solution.py:248
  120.8 1.9 %collective-permute-start.9 = (bf16[2,16,8,2,16,128]{5,4,3,2,1,0:T(8,128)(2,1)S(1)}, bf16[2,16,8,2,16,128]{5,4,3,2,1,0:T(8,128)(2,1)S(1)}, u32[]{:S(2)}, u32[]{:S(2)}) collective-permute-start(bf16[2,16,8,2,16,128]{5,4,3,2,1,0:T(8,128)(2,1)S(1)} %bitcast.6), channel_id=1, source_target_pairs={{0,16},{16,0},{32,48},{48,32},{64,80},{80,64},{96,112},{112,96},{1... | collective-permute-start | bytes 6291464 | tf_op jit(solution)/shard_map/ppermute | solution.py:221
  122.7 1.0 between.1
  123.7 7.7 %collective-permute-start.7 = (bf16[2,4,128,128]{3,2,1,0:T(8,128)(2,1)S(1)}, bf16[2,4,128,128]{3,2,1,0:T(8,128)(2,1)S(1)}, u32[]{:S(2)}, u32[]{:S(2)}) collective-permute-start(bf16[2,4,128,128]{3,2,1,0:T(8,128)(2,1)S(1)} %get-tuple-element.27), channel_id=1, source_target_pairs={{0,32},{16,48},{32,0},{48,16},{64,96},{80,112},{96,64},{112,80},{1... | collective-permute-start | bytes 786440 | tf_op jit(solution)/shard_map/ppermute | solution.py:221
  131.4 4.3 %collective-permute-start.8 = (bf16[2,4,128,128]{3,2,1,0:T(8,128)(2,1)S(1)}, bf16[2,4,128,128]{3,2,1,0:T(8,128)(2,1)S(1)}, u32[]{:S(2)}, u32[]{:S(2)}) collective-permute-start(bf16[2,4,128,128]{3,2,1,0:T(8,128)(2,1)S(1)} %get-tuple-element.28), channel_id=1, source_target_pairs={{0,96},{16,112},{32,64},{48,80},{64,32},{80,48},{96,0},{112,16},{1... | collective-permute-start | bytes 786440 | tf_op jit(solution)/shard_map/ppermute | solution.py:221
  135.7 0.0 collective-permute-done.9.own_swapped.far_swapped
  135.7 5.2 %rounds.1.base = bf16[4,2,8,128,128]{4,3,2,1,0:T(8,128)(2,1)} custom-call(s32[3]{0:T(128)S(1)} %pad_add_fusion.position, bf16[2,16,8,2,16,128]{5,4,3,2,1,0:T(8,128)(2,1)S(1)} %bitcast.8, bf16[2,16,8,2,16,128]{5,4,3,2,1,0:T(8,128)(2,1)S(1)} %bitcast.9, bf16[2,16,8,2,16,128]{5,4,3,2,1,0:T(8,128)(2,1)S(1)} %collective-permute-done.9.own_swapped.far_swapped, ...), custom_call_target="tpu_custom_call" | custom-call | tf_op jit(solution)/shard_map/rounds/pallas_call | solution.py:152
  140.9 8.5 %collective-permute-done.7.first = bf16[2,4,128,128]{3,2,1,0:T(8,128)(2,1)S(1)} collective-permute-done((bf16[2,4,128,128]{3,2,1,0:T(8,128)(2,1)S(1)}, bf16[2,4,128,128]{3,2,1,0:T(8,128)(2,1)S(1)}, u32[]{:S(2)}, u32[]{:S(2)}) %collective-permute-start.7) | collective-permute-done | bytes 262176 | tf_op jit(solution)/shard_map/ppermute | solution.py:221
  149.4 10.7 %collective-permute-done.8.second = bf16[2,4,128,128]{3,2,1,0:T(8,128)(2,1)S(1)} collective-permute-done((bf16[2,4,128,128]{3,2,1,0:T(8,128)(2,1)S(1)}, bf16[2,4,128,128]{3,2,1,0:T(8,128)(2,1)S(1)}, u32[]{:S(2)}, u32[]{:S(2)}) %collective-permute-start.8) | collective-permute-done | bytes 262176 | tf_op jit(solution)/shard_map/ppermute | solution.py:221
  160.1 1.4 place.1
  (8 shorter events, 0.1 us)
Async XLA Ops:
  6.9 113.9 %all-to-all-start = ((bf16[32,8,2,16,128]{4,3,2,1,0:T(8,128)(2,1)}), bf16[32,8,2,16,128]{4,3,2,1,0:T(8,128)(2,1)S(1)}, u32[]{:S(2)}, u32[]{:S(2)}) async-start(bf16[32,8,2,16,128]{4,3,2,1,0:T(8,128)(2,1)} %bitcast.10), calls=%async_computation | async-start | bytes 4194304 | tf_op jit(solution)/shard_map/all_to_all | solution.py:248
  22.5 12.4 %collective-permute-start = (bf16[4,4,2,16,128]{4,3,2,1,0:T(8,128)(2,1)S(1)}, bf16[4,4,2,16,128]{4,3,2,1,0:T(8,128)(2,1)S(1)}, u32[]{:S(2)}, u32[]{:S(2)}) collective-permute-start(bf16[4,4,2,16,128]{4,3,2,1,0:T(8,128)(2,1)S(1)} %get-tuple-element.19), channel_id=1, source_target_pairs={{0,1},{1,0},{2,3},{3,2},{4,5},{5,4},{6,7},{7,6},{8,9},{9,8},{10,11... | collective-permute-start | bytes 393224 | tf_op jit(solution)/shard_map/ppermute | solution.py:229
  25.3 13.9 %collective-permute-start.1 = (bf16[4,4,2,16,128]{4,3,2,1,0:T(8,128)(2,1)S(1)}, bf16[4,4,2,16,128]{4,3,2,1,0:T(8,128)(2,1)S(1)}, u32[]{:S(2)}, u32[]{:S(2)}) collective-permute-start(bf16[4,4,2,16,128]{4,3,2,1,0:T(8,128)(2,1)S(1)} %get-tuple-element.20), channel_id=1, source_target_pairs={{0,2},{1,3},{2,0},{3,1},{4,6},{5,7},{6,4},{7,5},{8,10},{9,11},{10,... | collective-permute-start | bytes 393224 | tf_op jit(solution)/shard_map/ppermute | solution.py:229
  28.1 13.8 %collective-permute-start.2 = (bf16[4,4,2,16,128]{4,3,2,1,0:T(8,128)(2,1)S(1)}, bf16[4,4,2,16,128]{4,3,2,1,0:T(8,128)(2,1)S(1)}, u32[]{:S(2)}, u32[]{:S(2)}) collective-permute-start(bf16[4,4,2,16,128]{4,3,2,1,0:T(8,128)(2,1)S(1)} %get-tuple-element.21), channel_id=1, source_target_pairs={{0,3},{1,2},{2,1},{3,0},{4,7},{5,6},{6,5},{7,4},{8,11},{9,10},{10,... | collective-permute-start | bytes 393224 | tf_op jit(solution)/shard_map/ppermute | solution.py:229
  41.9 65.9 %collective-permute-start.3 = (bf16[4,4,2,16,128]{4,3,2,1,0:T(8,128)(2,1)S(1)}, bf16[4,4,2,16,128]{4,3,2,1,0:T(8,128)(2,1)S(1)}, u32[]{:S(2)}, u32[]{:S(2)}) collective-permute-start(bf16[4,4,2,16,128]{4,3,2,1,0:T(8,128)(2,1)S(1)} %pad_maximum_fusion), channel_id=1, source_target_pairs={{0,96},{1,97},{2,98},{3,99},{4,100},{5,101},{6,102},{7,103},{8,104... | collective-permute-start | bytes 393224 | tf_op jit(solution)/shard_map/ppermute | solution.py:229
  47.6 60.1 %collective-permute-start.4 = (bf16[4,4,2,16,128]{4,3,2,1,0:T(8,128)(2,1)S(1)}, bf16[4,4,2,16,128]{4,3,2,1,0:T(8,128)(2,1)S(1)}, u32[]{:S(2)}, u32[]{:S(2)}) collective-permute-start(bf16[4,4,2,16,128]{4,3,2,1,0:T(8,128)(2,1)S(1)} %pad_maximum_fusion.1), channel_id=1, source_target_pairs={{0,100},{1,101},{2,102},{3,103},{4,96},{5,97},{6,98},{7,99},{8,108... | collective-permute-start | bytes 393224 | tf_op jit(solution)/shard_map/ppermute | solution.py:229
  51.1 56.6 %collective-permute-start.5 = (bf16[4,4,2,16,128]{4,3,2,1,0:T(8,128)(2,1)S(1)}, bf16[4,4,2,16,128]{4,3,2,1,0:T(8,128)(2,1)S(1)}, u32[]{:S(2)}, u32[]{:S(2)}) collective-permute-start(bf16[4,4,2,16,128]{4,3,2,1,0:T(8,128)(2,1)S(1)} %pad_maximum_fusion.2), channel_id=1, source_target_pairs={{0,104},{1,105},{2,106},{3,107},{4,108},{5,109},{6,110},{7,111},{8... | collective-permute-start | bytes 393224 | tf_op jit(solution)/shard_map/ppermute | solution.py:229
  61.9 45.8 %collective-permute-start.6 = (bf16[4,4,2,16,128]{4,3,2,1,0:T(8,128)(2,1)S(1)}, bf16[4,4,2,16,128]{4,3,2,1,0:T(8,128)(2,1)S(1)}, u32[]{:S(2)}, u32[]{:S(2)}) collective-permute-start(bf16[4,4,2,16,128]{4,3,2,1,0:T(8,128)(2,1)S(1)} %pad_maximum_fusion.3), channel_id=1, source_target_pairs={{0,108},{1,109},{2,110},{3,111},{4,104},{5,105},{6,106},{7,107},{8... | collective-permute-start | bytes 393224 | tf_op jit(solution)/shard_map/ppermute | solution.py:229
  120.8 14.9 %collective-permute-start.9 = (bf16[2,16,8,2,16,128]{5,4,3,2,1,0:T(8,128)(2,1)S(1)}, bf16[2,16,8,2,16,128]{5,4,3,2,1,0:T(8,128)(2,1)S(1)}, u32[]{:S(2)}, u32[]{:S(2)}) collective-permute-start(bf16[2,16,8,2,16,128]{5,4,3,2,1,0:T(8,128)(2,1)S(1)} %bitcast.6), channel_id=1, source_target_pairs={{0,16},{16,0},{32,48},{48,32},{64,80},{80,64},{96,112},{112,96},{1... | collective-permute-start | bytes 6291464 | tf_op jit(solution)/shard_map/ppermute | solution.py:221
  123.7 25.7 %collective-permute-start.7 = (bf16[2,4,128,128]{3,2,1,0:T(8,128)(2,1)S(1)}, bf16[2,4,128,128]{3,2,1,0:T(8,128)(2,1)S(1)}, u32[]{:S(2)}, u32[]{:S(2)}) collective-permute-start(bf16[2,4,128,128]{3,2,1,0:T(8,128)(2,1)S(1)} %get-tuple-element.27), channel_id=1, source_target_pairs={{0,32},{16,48},{32,0},{48,16},{64,96},{80,112},{96,64},{112,80},{1... | collective-permute-start | bytes 786440 | tf_op jit(solution)/shard_map/ppermute | solution.py:221
  131.4 28.7 %collective-permute-start.8 = (bf16[2,4,128,128]{3,2,1,0:T(8,128)(2,1)S(1)}, bf16[2,4,128,128]{3,2,1,0:T(8,128)(2,1)S(1)}, u32[]{:S(2)}, u32[]{:S(2)}) collective-permute-start(bf16[2,4,128,128]{3,2,1,0:T(8,128)(2,1)S(1)} %get-tuple-element.28), channel_id=1, source_target_pairs={{0,96},{16,112},{32,64},{48,80},{64,32},{80,48},{96,0},{112,16},{1... | collective-permute-start | bytes 786440 | tf_op jit(solution)/shard_map/ppermute | solution.py:221
